TPU v7x, 32 devices: a whole 2x2x4 slice. The times are simulated.
32 devices in a mesh: groups: 2 (over x), tensor: 16 (over z, y, core).
Axes of the slice: x: 2, y: 2, z: 4, core: 2. Of those that a mesh axis runs over, the one named last changes fastest.
Arguments:
- tokens: bfloat16 [512, 8192], P(('groups', 'tensor')), parts along dimension 0, may hold values from -6 to 6
- gate_weight: bfloat16 [8192, 16384], P(None, 'tensor'), may hold values from -0.0625 to 0.0625
- up_weight: bfloat16 [8192, 16384], P(None, 'tensor'), may hold values from -0.0625 to 0.0625
- adapter_down_weight: bfloat16 [32, 64, 8192], P(('groups', 'tensor')), parts along dimension 0, may hold values from -0.0625 to 0.0625
- adapter_up_weight: bfloat16 [32, 64, 16384], P(('groups', 'tensor')), parts along dimension 0, may hold values from -0.75 to 0.75
- row_adapter: int32 [512], P('groups'), parts along dimension 0, may hold values from 0 to 15, as said below
- sorted_rows: int32 [512], P('groups'), parts along dimension 0, may hold values from 0 to 255, as said below
- segment_count: int32 [32], P('groups'), parts along dimension 0, may hold values from 1 to 64, as said below
Outputs:
- hidden: bfloat16 [512, 16384], P('groups', 'tensor'), parts along dimension 0
There are 2 independent parts, one for each index of `groups`. A program takes and returns all parts, laid end to end along the dimension named above; an argument that names none is the same for every part. Nothing has to cross between parts.
Inputs may be any that keep to these rules, and one draw needn't show every extreme that they name: Row r uses adapter row_adapter[r]; adapter j is used by segment_count[j] rows. `sorted_rows`: a permutation of the rows; the rows of adapter j stand at positions seg_start[j] to seg_start[j] + segment_count[j] - 1. `segment_count`: the counts sum to 256; some adapter has exactly 64 rows.
All inputs are finite; a program needn't handle non-finite values.
Results may differ from a plain program's by a relative error of at most 0.0036.
Values may be sent and summed in bfloat16 or wider, within the bound.
No kernel may reach another device: no remote copies, remote signals or barrier semaphores. Data moves between devices by JAX's collectives and lax.ppermute only.
A program may use at most 128 MiB of HBM per device.

v0:
```python
import functools

import jax
import jax.numpy as jnp
from jax import lax
from jax.experimental import pallas as pl
from jax.experimental.pallas import tpu as pltpu
from jax.sharding import PartitionSpec as P

ADAPTER_SCALE = 0.5
ROWS_PER_LIMIT = 64
SLOT_SIZES = (80, 96)
CORES = 2
MIB = 1024 * 1024


def chip_ring(chips):
    return list(range(0, chips, 2)) + list(range(chips - 1, 0, -2))


def ring_chip(me, chips, distance):
    chip = me // CORES
    place = jnp.where(chip % 2 == 0, chip // 2, chips // 2 + (chips - 1 - chip) // 2)
    place = (place + distance + chips) % chips
    return jnp.where(place < chips // 2, 2 * place, chips - 1 - 2 * (place - chips // 2))


def ring_gather(block, axis, beside):
    size = lax.axis_size(axis)
    chips = size // CORES
    ring = chip_ring(chips)

    def moved(value, shift):
        pairs = [
            (ring[p] * CORES + k, ring[(p + shift) % chips] * CORES + k)
            for p in range(chips)
            for k in range(CORES)
        ]
        return lax.ppermute(value, axis, pairs)

    right, left = moved(block, 1), moved(block, -1)
    pieces = [(block, 0, 0), (right, 0, -1), (left, 0, 1)]
    half = block.shape[1] // 2
    far = chips // 2
    columns = (0, half), (half, 0)
    held = [(right[:, a : a + half], left[:, b : b + half]) for a, b in columns]
    held = beside(1, held)
    for step in range(2, far + 1):
        for chain in range(1 if step == far else 2):
            right, left = held[chain]
            held[chain] = moved(right, 1), moved(left, -1)
            for value, column, distance in zip(held[chain], columns[chain], (-step, step)):
                pieces.append((value, column, distance))
        held = beside(step, held)
    return pieces


ANY_SPEC = pl.BlockSpec(memory_space=pl.ANY)


def in_hbm(values):
    return [pltpu.with_memory_space_constraint(value, pltpu.HBM) for value in values]


def run_copies(copies):
    for copy in copies:
        copy.start()
    for copy in copies:
        copy.wait()


def make_plan(sizes, counts, sorted_ref, held_ref, choice_ref):
    chips, most = held_ref.shape
    rows = sorted_ref.shape[1]
    adapters = counts[0].shape[0] // chips

    def total(group, chip):
        return functools.reduce(jnp.add, [counts[group][chip * adapters + a] for a in range(adapters)])

    listed = jnp.broadcast_to(sorted_ref[...], (8, rows))
    slot = lax.broadcasted_iota(jnp.int32, (8, most), 1)
    start = jnp.int32(0)
    for chip in range(chips):
        turned = pltpu.roll(listed, (rows - start) % rows, 1)
        held_ref[chip : chip + 1, :] = jnp.where(slot < total(0, chip), turned[:, :most], -1)[0:1]
        start += total(0, chip)
    largest = functools.reduce(
        jnp.maximum, [total(group, chip) for group in range(len(counts)) for chip in range(chips)]
    )
    choice_ref[0] = functools.reduce(jnp.add, [(largest > size).astype(jnp.int32) for size in sizes[:-1]])


def down_copies(core, own_down_ref, other_down_ref, down_vmem, sems):
    ranks = own_down_ref.shape[0]
    return [
        pltpu.make_async_copy(ref, down_vmem.at[pl.ds(pl.multiple_of(where * ranks, ranks), ranks)], sems.at[i])
        for i, (ref, where) in enumerate(((own_down_ref, core), (other_down_ref, 1 - core)))
    ]


def shrink_near_kernel(sizes, places, groups, me, *refs):
    counts, refs = refs[:groups], refs[groups:]
    sorted_ref, own_down_ref, other_down_ref = refs[:3]
    refs = refs[3:]
    piece_refs = refs[: len(places)]
    tokens_ref, shrunk_ref, held_ref, choice_ref, tokens_vmem, down_vmem, sems = refs[len(places) :]
    chips = held_ref.shape[0]
    copies = down_copies(me[0] % CORES, own_down_ref, other_down_ref, down_vmem, sems)
    for ref, (column, distance) in zip(piece_refs, places):
        rows, width = ref.shape
        start = pl.multiple_of(ring_chip(me[0], chips, distance) * rows, rows)
        copies.append(
            pltpu.make_async_copy(
                ref, tokens_vmem.at[pl.ds(start, rows), pl.ds(column, width)], sems.at[len(copies)]
            )
        )
    for copy in copies:
        copy.start()
    make_plan(sizes, counts, sorted_ref, held_ref, choice_ref)
    for copy in copies:
        copy.wait()
    out_copy = pltpu.make_async_copy(tokens_vmem, tokens_ref, sems.at[len(copies)])
    out_copy.start()
    shrunk_ref[...] = lax.dot_general(
        tokens_vmem[...], down_vmem[...], (((1,), (1,)), ((), ())), preferred_element_type=jnp.float32
    ).astype(shrunk_ref.dtype)
    out_copy.wait()


def shrink_far_kernel(places, me, tokens_in, shrunk_in, own_down_ref, other_down_ref, *refs):
    piece_refs = refs[: len(places)]
    tokens_ref, shrunk_ref, far_vmem, down_vmem, sems = refs[len(places) :]
    rows, half = piece_refs[0].shape
    chips = tokens_in.shape[0] // rows
    slots = {distance % chips: i for i, distance in enumerate(range(chips // 2 - 1, chips // 2 + 2))}
    copies = down_copies(me[0] % CORES, own_down_ref, other_down_ref, down_vmem, sems)
    for ref, (column, distance) in zip(piece_refs, places):
        slot = slots[distance % chips]
        copies.append(
            pltpu.make_async_copy(
                ref, far_vmem.at[pl.ds(slot * rows, rows), pl.ds(column, half)], sems.at[len(copies)]
            )
        )
    run_copies(copies)
    starts = [pl.multiple_of(ring_chip(me[0], chips, distance) * rows, rows) for distance in slots]
    out_copies = [
        pltpu.make_async_copy(
            far_vmem.at[pl.ds(i * rows, rows)], tokens_ref.at[pl.ds(start, rows)], sems.at[len(copies) + i]
        )
        for i, start in enumerate(starts)
    ]
    for copy in out_copies:
        copy.start()
    shrunk = lax.dot_general(
        far_vmem[...], down_vmem[...], (((1,), (1,)), ((), ())), preferred_element_type=jnp.float32
    ).astype(shrunk_ref.dtype)
    shrunk_ref[...] = shrunk_in[...]
    for i, start in enumerate(starts):
        shrunk_ref[pl.ds(start, rows), :] = shrunk[i * rows : (i + 1) * rows]
    for copy in out_copies:
        copy.wait()


def shrink(me, counts, sorted_rows, pieces, own_down, other_down, sizes):
    ranks, width = own_down.shape
    rows_all = sorted_rows.shape[0]
    rows = rows_all // CORES
    values = [value for value, _, _ in pieces]
    near = values[:-6]
    block = values[0].shape[0]
    tokens_shape = pltpu.HBM((rows, width), jnp.bfloat16)
    shrunk_shape = jax.ShapeDtypeStruct((rows, CORES * ranks), jnp.bfloat16)
    held_shape = jax.ShapeDtypeStruct((rows // block, sizes[-1]), jnp.int32)

    def whole(shape):
        return pl.BlockSpec(shape, lambda i, *_: (0, 0))

    down_vmem = pltpu.VMEM((CORES * ranks, width), jnp.bfloat16)
    downs = in_hbm([own_down]) + [other_down]
    tokens, shrunk, held, choice = pl.pallas_call(
        functools.partial(shrink_near_kernel, sizes, [place[1:] for place in pieces[:-6]], len(counts)),
        grid_spec=pltpu.PrefetchScalarGridSpec(
            num_scalar_prefetch=1 + len(counts),
            grid=(1,),
            in_specs=[whole((1, rows_all))] + [ANY_SPEC] * (2 + len(near)),
            out_specs=[
                ANY_SPEC,
                whole(shrunk_shape.shape),
                whole(held_shape.shape),
                pl.BlockSpec(memory_space=pltpu.SMEM),
            ],
            scratch_shapes=[
                pltpu.VMEM((rows, width), jnp.bfloat16),
                down_vmem,
                pltpu.SemaphoreType.DMA((3 + len(near),)),
            ],
        ),
        out_shape=[tokens_shape, shrunk_shape, held_shape, jax.ShapeDtypeStruct((1,), jnp.int32)],
        compiler_params=pltpu.CompilerParams(vmem_limit_bytes=rows * width * 2 + 16 * MIB),
        name="shrink_near",
    )(me, *counts, *in_hbm([sorted_rows.reshape(1, rows_all)]), *downs, *in_hbm(near[:1]), *near[1:])
    tokens, shrunk = pl.pallas_call(
        functools.partial(shrink_far_kernel, [place[1:] for place in pieces[-6:]]),
        grid_spec=pltpu.PrefetchScalarGridSpec(
            num_scalar_prefetch=1,
            grid=(1,),
            in_specs=[ANY_SPEC, whole(shrunk_shape.shape)] + [ANY_SPEC] * 8,
            out_specs=[ANY_SPEC, whole(shrunk_shape.shape)],
            scratch_shapes=[
                pltpu.VMEM((3 * block, width), jnp.bfloat16),
                down_vmem,
                pltpu.SemaphoreType.DMA((11,)),
            ],
        ),
        out_shape=[tokens_shape, shrunk_shape],
        input_output_aliases={1: 0},
        compiler_params=pltpu.CompilerParams(vmem_limit_bytes=16 * MIB),
        name="shrink_far",
    )(me, *in_hbm([tokens]), shrunk, *downs, *values[-6:])
    return tokens, shrunk, held, choice


def expand_kernel(order, block, counts, me, held_ref, own_ref, other_ref, keep_ref, got_ref, out_ref, maps_vmem, out_vmem, sems):
    chips, slots, units = out_vmem.shape
    most = held_ref.shape[1]
    ranks = keep_ref.shape[0]
    adapters = counts.shape[0] // chips
    chip = me[0] // CORES
    core = me[0] % CORES
    copies = []
    for c in range(chips):
        start = pl.multiple_of((order[c] * CORES + core) * units, units)
        for ref, where in ((keep_ref, core), (got_ref, 1 - core)):
            copies.append(
                pltpu.make_async_copy(
                    ref.at[:, pl.ds(start, units)],
                    maps_vmem.at[c, pl.ds(pl.multiple_of(where * ranks, ranks), ranks)],
                    sems.at[len(copies)],
                )
            )
    for copy in copies:
        copy.start()

    wanted = held_ref[pl.ds(chip, 1), :]
    index = lax.broadcasted_iota(jnp.int32, (own_ref.shape[0], most), 0)
    row = index // block * (CORES * block) + index % block
    picked = jnp.zeros((most, own_ref.shape[1]), jnp.float32)
    for ref, where in ((own_ref, core), (other_ref, 1 - core)):
        hit = (row + where * block == wanted).astype(jnp.float32).astype(jnp.bfloat16)
        picked += lax.dot_general(hit, ref[...], (((0,), (0,)), ((), ())), preferred_element_type=jnp.float32)
    slot = lax.broadcasted_iota(jnp.int32, picked.shape, 0)
    adapter = lax.broadcasted_iota(jnp.int32, picked.shape, 1) // (picked.shape[1] // adapters)
    mine = jnp.zeros(picked.shape, jnp.int32)
    first = jnp.int32(0)
    for a in range(adapters):
        end = first + counts[chip * adapters + a]
        mine += ((adapter == a) & (slot >= first) & (slot < end)).astype(jnp.int32)
        first = end
    shrunk = jnp.where(mine > 0, picked, 0.0).astype(jnp.bfloat16)[:slots]

    out_copies = []
    for c in range(chips):
        copies[2 * c].wait()
        copies[2 * c + 1].wait()
        product = jnp.dot(shrunk, maps_vmem[c], preferred_element_type=jnp.float32)
        out_vmem[c] = (ADAPTER_SCALE * product).astype(out_vmem.dtype)
        out_copies.append(pltpu.make_async_copy(out_vmem.at[c], out_ref.at[c], sems.at[2 * chips + c]))
        out_copies[-1].start()
    for copy in out_copies:
        copy.wait()


def expand(counts, me, held, own_shrunk, other_shrunk, keep, got, order, slots, block):
    ranks, columns = keep.shape
    chips, most = held.shape
    units = columns // chips // CORES
    rows, ranks_all = own_shrunk.shape
    shrunk_spec = pl.BlockSpec((rows, ranks_all), lambda i, s, t: (0, 0))
    return pl.pallas_call(
        functools.partial(expand_kernel, order, block),
        grid_spec=pltpu.PrefetchScalarGridSpec(
            num_scalar_prefetch=2,
            grid=(1,),
            in_specs=[
                pl.BlockSpec((chips, most), lambda i, s, t: (0, 0)),
                shrunk_spec,
                shrunk_spec,
                ANY_SPEC,
                ANY_SPEC,
            ],
            out_specs=ANY_SPEC,
            scratch_shapes=[
                pltpu.VMEM((chips, ranks_all, units), jnp.bfloat16),
                pltpu.VMEM((chips, slots, units), jnp.bfloat16),
                pltpu.SemaphoreType.DMA((3 * chips,)),
            ],
        ),
        out_shape=pltpu.HBM((chips, slots, units), jnp.bfloat16),
        compiler_params=pltpu.CompilerParams(vmem_limit_bytes=16 * MIB),
        cost_estimate=pl.CostEstimate(
            flops=2 * slots * ranks_all * chips * units,
            bytes_accessed=2 * (slots + ranks_all) * chips * units,
            transcendentals=0,
        ),
        name="expand",
    )(counts, me, held, own_shrunk, other_shrunk, *in_hbm([keep, got]))


def project_kernel(block, me, gate_weight_ref, up_weight_ref, own_ref, other_ref, gate_ref, up_ref, tokens_vmem, sems):
    depth = gate_weight_ref.shape[0]
    core = me[0] % CORES
    k = pl.program_id(0)

    @pl.when(k == 0)
    def _():
        copies = []
        for ref, where in ((own_ref, core), (other_ref, 1 - core)):
            for chip in range(ref.shape[0] // block):
                start = pl.multiple_of((chip * CORES + where) * block, block)
                copies.append(
                    pltpu.make_async_copy(
                        ref.at[pl.ds(chip * block, block)], tokens_vmem.at[pl.ds(start, block)], sems.at[len(copies)]
                    )
                )
        run_copies(copies)
        gate_ref[...] = jnp.zeros_like(gate_ref)
        up_ref[...] = jnp.zeros_like(up_ref)

    tokens = tokens_vmem[:, pl.ds(pl.multiple_of(k * depth, depth), depth)]
    gate_ref[...] += jnp.dot(tokens, gate_weight_ref[...], preferred_element_type=jnp.float32)
    up_ref[...] += jnp.dot(tokens, up_weight_ref[...], preferred_element_type=jnp.float32)

    @pl.when(k == pl.num_programs(0) - 1)
    def _():
        gate = gate_ref[...]
        gate_ref[...] = gate / (1.0 + jnp.exp(-gate))


def project(me, own, other, gate_weight, up_weight, block):
    width, units = gate_weight.shape
    rows = CORES * own.shape[0]
    depth = min(1024, width)
    weight_spec = pl.BlockSpec((depth, units), lambda k, s: (k, 0))
    out_spec = pl.BlockSpec((rows, units), lambda k, s: (0, 0))
    out = pltpu.HBM((rows, units), jnp.float32)
    return pl.pallas_call(
        functools.partial(project_kernel, block),
        grid_spec=pltpu.PrefetchScalarGridSpec(
            num_scalar_prefetch=1,
            grid=(width // depth,),
            in_specs=[weight_spec, weight_spec, ANY_SPEC, ANY_SPEC],
            out_specs=[out_spec, out_spec],
            scratch_shapes=[
                pltpu.VMEM((rows, width), jnp.bfloat16),
                pltpu.SemaphoreType.DMA((rows // block,)),
            ],
        ),
        out_shape=[out, out],
        compiler_params=pltpu.CompilerParams(vmem_limit_bytes=rows * width * 2 + 20 * MIB),
        cost_estimate=pl.CostEstimate(
            flops=4 * rows * width * units,
            bytes_accessed=2 * (rows + 2 * units) * width,
            transcendentals=rows * units,
        ),
        name="project",
    )(me, *in_hbm([gate_weight, up_weight, own, other]))


def combine_kernel(pick_ref, gate_ref, up_ref, products_ref, out_ref):
    delta = jnp.dot(pick_ref[...], products_ref[...], preferred_element_type=jnp.float32)
    out_ref[...] = (gate_ref[...] * (up_ref[...] + delta)).astype(out_ref.dtype)


def combine(pick, gate, up, products):
    rows, units = gate.shape
    slots_all = products.shape[0]
    tile = min(512, units)
    column_spec = pl.BlockSpec((rows, tile), lambda n: (0, n))
    return pl.pallas_call(
        combine_kernel,
        grid=(units // tile,),
        in_specs=[
            pl.BlockSpec((rows, slots_all), lambda n: (0, 0)),
            column_spec,
            column_spec,
            pl.BlockSpec((slots_all, tile), lambda n: (0, n)),
        ],
        out_specs=column_spec,
        out_shape=pltpu.HBM((rows, units), jnp.bfloat16),
        compiler_params=pltpu.CompilerParams(vmem_limit_bytes=rows * slots_all * 4 + 20 * MIB),
        cost_estimate=pl.CostEstimate(
            flops=2 * rows * slots_all * units, bytes_accessed=10 * rows * units, transcendentals=0
        ),
        name="combine",
    )(*in_hbm([pick, gate, up]), products)


def per_device(
    tokens,
    gate_weight,
    up_weight,
    adapter_down_weight,
    adapter_up_weight,
    row_adapter,
    sorted_rows,
    segment_count,
):
    axis = "tensor"
    size = lax.axis_size(axis)
    me = lax.axis_index(axis).astype(jnp.int32)
    chips = size // CORES
    resident, rank, width = adapter_down_weight.shape
    ranks = resident * rank
    rows = row_adapter.shape[0]
    block = tokens.shape[0]
    me_array = me.reshape(1)
    flips = [(d, d ^ 1) for d in range(size)]

    def other_core(value):
        return lax.ppermute(value, axis, flips)

    most = CORES * resident * ROWS_PER_LIMIT
    sizes = [slots for slots in SLOT_SIZES if slots < most] + [most]
    groups = lax.axis_size("groups")
    own_down = adapter_down_weight.reshape(ranks, width)
    own_maps = adapter_up_weight.reshape(ranks, -1)
    other_down = other_core(own_down)
    counts = [segment_count] + [
        lax.ppermute(segment_count, "groups", [(g, (g + shift) % groups) for g in range(groups)])
        for shift in range(1, groups)
    ]
    other_maps = other_core(own_maps)

    def beside(step, values):
        nonlocal other_down, counts, other_maps
        if step == 1:
            other_down, counts, values[0], values[1] = lax.optimization_barrier((other_down, counts, *values))
        return values

    pieces = ring_gather(tokens, axis, beside)
    own_tokens, own_shrunk, held, choice = shrink(
        me_array, counts, sorted_rows, pieces, own_down, other_down, sizes
    )
    other_shrunk = other_core(own_shrunk)

    order = [half * (chips // 2) + c for c in range(chips // 2) for half in range(2)]
    same_core = [[c * CORES + k for c in order] for k in range(CORES)]

    def finish(slots):
        def branch(own_tokens, own_shrunk, other_shrunk, own_maps, other_maps, held, gate_weight, up_weight):
            products = expand(
                segment_count, me_array, held, own_shrunk, other_shrunk, own_maps, other_maps, order, slots, block
            )
            products = lax.all_to_all(
                products, axis, split_axis=0, concat_axis=0, axis_index_groups=same_core, tiled=True
            )
            held, other_tokens = lax.optimization_barrier((held, other_core(own_tokens)))
            held_rows = jnp.stack([held[c, :slots] for c in order]).reshape(1, chips * slots)
            pick = (jnp.arange(rows, dtype=jnp.int32)[:, None] == held_rows).astype(jnp.bfloat16)
            pick, other_tokens = lax.optimization_barrier((pick, other_tokens))
            gate, up = project(me_array, own_tokens, other_tokens, gate_weight, up_weight, block)
            return combine(pick, gate, up, products.reshape(chips * slots, -1))

        return branch

    return lax.switch(
        choice[0],
        [finish(slots) for slots in sizes],
        own_tokens,
        own_shrunk,
        other_shrunk,
        own_maps,
        other_maps,
        held,
        gate_weight,
        up_weight,
    )


def solution(mesh):
    placed = (
        P(("groups", "tensor"), None),
        P(None, "tensor"),
        P(None, "tensor"),
        P(("groups", "tensor"), None, None),
        P(("groups", "tensor"), None, None),
        P("groups"),
        P("groups"),
        P("groups"),
    )
    return jax.shard_map(
        per_device, mesh=mesh, in_specs=placed, out_specs=P("groups", "tensor"), check_vma=False
    )
```

profile of v0, /device:TPU:0, one launch (start us, length us, event | category | flops | bytes accessed | tf_op | source)
XLA Modules:
  0.0 80.9 jit_solution(18087701004981721972)
XLA Ops:
  0.0 3.0 %collective-permute-start.5 = (bf16[16,8192]{1,0:T(8,128)(2,1)}, bf16[16,8192]{1,0:T(8,128)(2,1)S(1)}, u32[]{:S(2)}, u32[]{:S(2)}) collective-permute-start(bf16[16,8192]{1,0:T(8,128)(2,1)} %refs_5_.1), channel_id=1, source_target_pairs={{0,4},{1,5},{4,8},{5,9},{8,12},{9,13},{12,14},{13,15},{14,10},{15,... | collective-permute-start | bytes 786440 | tf_op jit(solution)/shard_map/ppermute | solution.py:39
  3.0 1.9 %collective-permute-start.4 = (s32[16]{0:T(128)}, s32[16]{0:T(128)S(1)}, u32[]{:S(2)}, u32[]{:S(2)}) collective-permute-start(s32[16]{0:T(128)} %refs_0_), channel_id=1, source_target_pairs={{0,16},{16,0},{1,17},{17,1},{2,18},{18,2},{3,19},{19,3},{4,20},{20... | collective-permute-start | bytes 200 | tf_op jit(solution)/shard_map/ppermute | solution.py:429
  5.0 0.5 collective-permute-start.18
  5.5 4.0 %collective-permute-done.5.refs_6_ = bf16[16,8192]{1,0:T(8,128)(2,1)S(1)} collective-permute-done((bf16[16,8192]{1,0:T(8,128)(2,1)}, bf16[16,8192]{1,0:T(8,128)(2,1)S(1)}, u32[]{:S(2)}, u32[]{:S(2)}) %collective-permute-start.5) | collective-permute-done | bytes 262176 | tf_op jit(solution)/shard_map/ppermute | solution.py:39
  9.5 1.5 %collective-permute-done.6.refs_7_ = bf16[16,8192]{1,0:T(8,128)(2,1)S(1)} collective-permute-done((bf16[16,8192]{1,0:T(8,128)(2,1)}, bf16[16,8192]{1,0:T(8,128)(2,1)S(1)}, u32[]{:S(2)}, u32[]{:S(2)}) %collective-permute-start.6) | collective-permute-done | bytes 262176 | tf_op jit(solution)/shard_map/ppermute | solution.py:39
  11.0 1.6 %collective-permute-start.7 = (bf16[16,4096]{1,0:T(8,128)(2,1)S(1)}, bf16[16,4096]{1,0:T(8,128)(2,1)S(1)}, u32[]{:S(2)}, u32[]{:S(2)}) collective-permute-start(bf16[16,4096]{1,0:T(8,128)(2,1)S(1)} %get-tuple-element.133), channel_id=1, source_target_pairs={{0,4},{1,5},{4,8},{5,9},{8,12},{9,13},{12,14},{13,15},{14,10},{15,... | collective-permute-start | bytes 393224 | tf_op jit(solution)/shard_map/ppermute | solution.py:39
  12.7 0.4 collective-permute-start.8
  13.1 1.6 %collective-permute-start.9 = (bf16[16,4096]{1,0:T(8,128)(2,1)S(1)}, bf16[16,4096]{1,0:T(8,128)(2,1)S(1)}, u32[]{:S(2)}, u32[]{:S(2)}) collective-permute-start(bf16[16,4096]{1,0:T(8,128)(2,1)S(1)} %get-tuple-element.135), channel_id=1, source_target_pairs={{0,4},{1,5},{4,8},{5,9},{8,12},{9,13},{12,14},{13,15},{14,10},{15,... | collective-permute-start | bytes 393224 | tf_op jit(solution)/shard_map/ppermute | solution.py:39
  14.7 0.4 collective-permute-start.10
  15.2 1.9 %collective-permute-done.7.refs_8_ = bf16[16,4096]{1,0:T(8,128)(2,1)S(1)} collective-permute-done((bf16[16,4096]{1,0:T(8,128)(2,1)S(1)}, bf16[16,4096]{1,0:T(8,128)(2,1)S(1)}, u32[]{:S(2)}, u32[]{:S(2)}) %collective-permute-start.7) | collective-permute-done | bytes 131104 | tf_op jit(solution)/shard_map/ppermute | solution.py:39
  17.0 1.6 %collective-permute-start.11 = (bf16[16,4096]{1,0:T(8,128)(2,1)S(1)}, bf16[16,4096]{1,0:T(8,128)(2,1)S(1)}, u32[]{:S(2)}, u32[]{:S(2)}) collective-permute-start(bf16[16,4096]{1,0:T(8,128)(2,1)S(1)} %collective-permute-done.7.refs_8_), channel_id=1, source_target_pairs={{0,4},{1,5},{4,8},{5,9},{8,12},{9,13},{12,14},{13,15},{14,10},{15,... | collective-permute-start | bytes 393224 | tf_op jit(solution)/shard_map/ppermute | solution.py:39
  18.6 0.5 collective-permute-start.12
  19.0 0.8 collective-permute-done.9.refs_10_
  19.8 1.6 %collective-permute-start.13 = (bf16[16,4096]{1,0:T(8,128)(2,1)S(1)}, bf16[16,4096]{1,0:T(8,128)(2,1)S(1)}, u32[]{:S(2)}, u32[]{:S(2)}) collective-permute-start(bf16[16,4096]{1,0:T(8,128)(2,1)S(1)} %collective-permute-done.9.refs_10_), channel_id=1, source_target_pairs={{0,4},{1,5},{4,8},{5,9},{8,12},{9,13},{12,14},{13,15},{14,10},{15,... | collective-permute-start | bytes 393224 | tf_op jit(solution)/shard_map/ppermute | solution.py:39
  21.4 0.5 collective-permute-start.14
  21.8 0.9 %collective-permute-done.11.refs_0_ = bf16[16,4096]{1,0:T(8,128)(2,1)S(1)} collective-permute-done((bf16[16,4096]{1,0:T(8,128)(2,1)S(1)}, bf16[16,4096]{1,0:T(8,128)(2,1)S(1)}, u32[]{:S(2)}, u32[]{:S(2)}) %collective-permute-start.11) | collective-permute-done | bytes 131104 | tf_op jit(solution)/shard_map/ppermute | solution.py:39
  22.7 1.6 %collective-permute-start.15 = (bf16[16,4096]{1,0:T(8,128)(2,1)S(1)}, bf16[16,4096]{1,0:T(8,128)(2,1)S(1)}, u32[]{:S(2)}, u32[]{:S(2)}) collective-permute-start(bf16[16,4096]{1,0:T(8,128)(2,1)S(1)} %collective-permute-done.11.refs_0_), channel_id=1, source_target_pairs={{0,4},{1,5},{4,8},{5,9},{8,12},{9,13},{12,14},{13,15},{14,10},{15,... | collective-permute-start | bytes 393224 | tf_op jit(solution)/shard_map/ppermute | solution.py:39
  24.3 0.5 collective-permute-start.16
  24.7 4.6 %shrink_near.1 = (bf16[128,8192]{1,0:T(8,128)(2,1)}, bf16[128,128]{1,0:T(8,128)(2,1)S(1)}, s32[8,128]{1,0:T(8,128)S(1)}, s32[1]{0:T(128)}) custom-call(s32[1]{0:T(128)} %bitcast.4.me, s32[16]{0:T(128)} %refs_0_, s32[16]{0:T(128)S(1)} %collective-permute-done.4.refs_1_, s32[1,256]{1,0:T(1,128)} %bitcast.20, bf16[64,8192]{1,0:T(8,128)(2,1)} %bitcast.17, ...), custom_call_target="tpu_custom_call" | custom-call | tf_op jit(solution)/shard_map/shrink_near/pallas_call | solution.py:180
  29.4 0.0 copy-start.1
  29.4 2.9 %shrink_far.1 = (bf16[128,8192]{1,0:T(8,128)(2,1)}, bf16[128,128]{1,0:T(8,128)(2,1)S(1)}) custom-call(s32[1]{0:T(128)} %bitcast.4.me, bf16[128,8192]{1,0:T(8,128)(2,1)} %get-tuple-element.138.tokens_in, bf16[128,128]{1,0:T(8,128)(2,1)S(1)} %get-tuple-element.139.shrunk_in, bf16[64,8192]{1,0:T(8,128)(2,1)} %bitcast.18, ...), custom_call_target="tpu_custom_call", output_to_operand_aliasing={{0}: (1, {})} | custom-call | tf_op jit(solution)/shard_map/shrink_far/pallas_call | solution.py:202
  32.3 0.1 collective-permute-start.17
  33.1 0.5 collective-permute-done.17
  33.6 47.3 %conditional.1 = (bf16[256,1024]{1,0:T(8,128)(2,1)}) conditional(s32[]{:T(128)} %bitcast.7, (bf16[128,8192]{1,0:T(8,128)(2,1)}, s32[8,128]{1,0:T(8,128)S(1)}, s32[1]{0:T(128)}, bf16[8192,1024]{1,0:T(8,128)(2,1)}, bf16[8192,1024]{1,0:T(8,128)(2,1)}, /*index=5*/s32[16]{0:T(128)S(1)}, bf16[128,128]{1,0:T(8,128)(2,1)S(1)}, ...), branch_computations={%region_0.0_spmd, %region_1.0_spmd, %region_2.0_spmd} | conditional | flops 9395765248 | bytes 64833132 | solution.py:466
  33.6 0.2 collective-permute-start.1
  33.8 4.1 %expand.4 = bf16[8,96,1024]{2,1,0:T(8,128)(2,1)} custom-call(s32[16]{0:T(128)S(1)} %get-tuple-element.96.counts, s32[1]{0:T(128)} %get-tuple-element.90.me, s32[8,128]{1,0:T(8,128)S(1)} %get-tuple-element.87.held_ref, bf16[128,128]{1,0:T(8,128)(2,1)S(1)} %get-tuple-element.97.own_ref, bf16[128,128]{1,0:T(8,128)(2,1)S(1)} %get-tuple-element.98.other_ref, ...), custom_call_target="tpu_custom_call" | custom-call | flops 201326592 | bytes 3670016 | tf_op jit(solution)/shard_map/cond/branch_1_fun/expand/pallas_call | solution.py:279
  37.9 5.1 %all-to-all-start.1 = ((bf16[8,96,1024]{2,1,0:T(8,128)(2,1)}), bf16[8,96,1024]{2,1,0:T(8,128)(2,1)S(1)}, u32[]{:S(2)}, u32[]{:S(2)}) async-start(bf16[8,96,1024]{2,1,0:T(8,128)(2,1)} %expand.4), calls=%async_computation.1 | async-start | bytes 3145728 | tf_op jit(solution)/shard_map/cond/branch_1_fun/all_to_all | solution.py:454
  43.0 0.1 eq.31
  43.1 0.8 %fusion.1.pick_ref = bf16[256,768]{1,0:T(8,128)(2,1)} fusion(s32[768]{0:T(1024)S(1)} %eq.31), kind=kLoop, calls=%fused_computation.3 | loop fusion | flops 393216 | bytes 396288 | tf_op jit(solution)/shard_map/cond/branch_1_fun/convert_element_type | solution.py:459
  43.9 20.2 %project.4 = (f32[256,1024]{1,0:T(8,128)}, f32[256,1024]{1,0:T(8,128)}) custom-call(s32[1]{0:T(128)} %get-tuple-element.90.me, bf16[8192,1024]{1,0:T(8,128)(2,1)} %get-tuple-element.151.gate_weight_ref, bf16[8192,1024]{1,0:T(8,128)(2,1)} %get-tuple-element.154.up_weight_ref, bf16[128,8192]{1,0:T(8,128)(2,1)} %get-tuple-element.86.own_ref, ...), custom_call_target="tpu_custom_call" | custom-call | flops 8589934592 | bytes 37748736 | tf_op jit(solution)/shard_map/cond/branch_1_fun/project/pallas_call | solution.py:346
  64.1 13.9 %all-to-all-done.1 = bf16[8,96,1024]{2,1,0:T(8,128)(2,1)S(1)} async-done(((bf16[8,96,1024]{2,1,0:T(8,128)(2,1)}), bf16[8,96,1024]{2,1,0:T(8,128)(2,1)S(1)}, u32[]{:S(2)}, u32[]{:S(2)}) %all-to-all-start.1) | async-done | bytes 1572896 | tf_op jit(solution)/shard_map/cond/branch_1_fun/all_to_all | solution.py:454
  78.1 2.8 %combine.4 = bf16[256,1024]{1,0:T(8,128)(2,1)} custom-call(bf16[256,768]{1,0:T(8,128)(2,1)} %fusion.1.pick_ref, f32[256,1024]{1,0:T(8,128)} %get-tuple-element.94.gate_ref, f32[256,1024]{1,0:T(8,128)} %get-tuple-element.95.up_ref, bf16[768,1024]{1,0:T(8,128)(2,1)S(1)} %bitcast.10), custom_call_target="tpu_custom_call" | custom-call | flops 402653184 | bytes 2621440 | tf_op jit(solution)/shard_map/cond/branch_1_fun/combine/pallas_call | solution.py:379
  (18 shorter events, 0.1 us)
Async XLA Ops:
  0.0 9.5 %collective-permute-start.5 = (bf16[16,8192]{1,0:T(8,128)(2,1)}, bf16[16,8192]{1,0:T(8,128)(2,1)S(1)}, u32[]{:S(2)}, u32[]{:S(2)}) collective-permute-start(bf16[16,8192]{1,0:T(8,128)(2,1)} %refs_5_.1), channel_id=1, source_target_pairs={{0,4},{1,5},{4,8},{5,9},{8,12},{9,13},{12,14},{13,15},{14,10},{15,... | collective-permute-start | bytes 786440 | tf_op jit(solution)/shard_map/ppermute | solution.py:39
  3.0 8.0 %collective-permute-start.6 = (bf16[16,8192]{1,0:T(8,128)(2,1)}, bf16[16,8192]{1,0:T(8,128)(2,1)S(1)}, u32[]{:S(2)}, u32[]{:S(2)}) collective-permute-start(bf16[16,8192]{1,0:T(8,128)(2,1)} %refs_5_.1), channel_id=1, source_target_pairs={{0,2},{1,3},{4,0},{5,1},{8,4},{9,5},{12,8},{13,9},{14,12},{15,13},... | collective-permute-start | bytes 786440 | tf_op jit(solution)/shard_map/ppermute | solution.py:39
  3.0 8.0 %collective-permute-start.4 = (s32[16]{0:T(128)}, s32[16]{0:T(128)S(1)}, u32[]{:S(2)}, u32[]{:S(2)}) collective-permute-start(s32[16]{0:T(128)} %refs_0_), channel_id=1, source_target_pairs={{0,16},{16,0},{1,17},{17,1},{2,18},{18,2},{3,19},{19,3},{4,20},{20... | collective-permute-start | bytes 200 | tf_op jit(solution)/shard_map/ppermute | solution.py:429
  5.0 6.1 %collective-permute-start.3 = (bf16[64,8192]{1,0:T(8,128)(2,1)}, bf16[64,8192]{1,0:T(8,128)(2,1)S(1)}, u32[]{:S(2)}, u32[]{:S(2)}) collective-permute-start(bf16[64,8192]{1,0:T(8,128)(2,1)} %bitcast.16), channel_id=1, source_target_pairs={{0,1},{1,0},{2,3},{3,2},{4,5},{5,4},{6,7},{7,6},{8,9},{9,8},{10,11... | collective-permute-start | bytes 3145736 | tf_op jit(solution)/shard_map/ppermute | solution.py:420
  5.0 28.6 %collective-permute-start.18 = (bf16[64,16384]{1,0:T(8,128)(2,1)}, bf16[64,16384]{1,0:T(8,128)(2,1)}, u32[]{:S(2)}, u32[]{:S(2)}) collective-permute-start(bf16[64,16384]{1,0:T(8,128)(2,1)} %bitcast.12), channel_id=1, source_target_pairs={{0,1},{1,0},{2,3},{3,2},{4,5},{5,4},{6,7},{7,6},{8,9},{9,8},{10,11... | collective-permute-start | bytes 6291464 | tf_op jit(solution)/shard_map/ppermute | solution.py:420
  11.0 6.0 %collective-permute-start.7 = (bf16[16,4096]{1,0:T(8,128)(2,1)S(1)}, bf16[16,4096]{1,0:T(8,128)(2,1)S(1)}, u32[]{:S(2)}, u32[]{:S(2)}) collective-permute-start(bf16[16,4096]{1,0:T(8,128)(2,1)S(1)} %get-tuple-element.133), channel_id=1, source_target_pairs={{0,4},{1,5},{4,8},{5,9},{8,12},{9,13},{12,14},{13,15},{14,10},{15,... | collective-permute-start | bytes 393224 | tf_op jit(solution)/shard_map/ppermute | solution.py:39
  12.7 5.9 %collective-permute-start.8 = (bf16[16,4096]{1,0:T(8,128)(2,1)S(1)}, bf16[16,4096]{1,0:T(8,128)(2,1)S(1)}, u32[]{:S(2)}, u32[]{:S(2)}) collective-permute-start(bf16[16,4096]{1,0:T(8,128)(2,1)S(1)} %get-tuple-element.134), channel_id=1, source_target_pairs={{0,2},{1,3},{4,0},{5,1},{8,4},{9,5},{12,8},{13,9},{14,12},{15,13},... | collective-permute-start | bytes 393224 | tf_op jit(solution)/shard_map/ppermute | solution.py:39
  13.1 6.7 %collective-permute-start.9 = (bf16[16,4096]{1,0:T(8,128)(2,1)S(1)}, bf16[16,4096]{1,0:T(8,128)(2,1)S(1)}, u32[]{:S(2)}, u32[]{:S(2)}) collective-permute-start(bf16[16,4096]{1,0:T(8,128)(2,1)S(1)} %get-tuple-element.135), channel_id=1, source_target_pairs={{0,4},{1,5},{4,8},{5,9},{8,12},{9,13},{12,14},{13,15},{14,10},{15,... | collective-permute-start | bytes 393224 | tf_op jit(solution)/shard_map/ppermute | solution.py:39
  14.7 6.7 %collective-permute-start.10 = (bf16[16,4096]{1,0:T(8,128)(2,1)S(1)}, bf16[16,4096]{1,0:T(8,128)(2,1)S(1)}, u32[]{:S(2)}, u32[]{:S(2)}) collective-permute-start(bf16[16,4096]{1,0:T(8,128)(2,1)S(1)} %get-tuple-element.136), channel_id=1, source_target_pairs={{0,2},{1,3},{4,0},{5,1},{8,4},{9,5},{12,8},{13,9},{14,12},{15,13},... | collective-permute-start | bytes 393224 | tf_op jit(solution)/shard_map/ppermute | solution.py:39
  17.0 5.7 %collective-permute-start.11 = (bf16[16,4096]{1,0:T(8,128)(2,1)S(1)}, bf16[16,4096]{1,0:T(8,128)(2,1)S(1)}, u32[]{:S(2)}, u32[]{:S(2)}) collective-permute-start(bf16[16,4096]{1,0:T(8,128)(2,1)S(1)} %collective-permute-done.7.refs_8_), channel_id=1, source_target_pairs={{0,4},{1,5},{4,8},{5,9},{8,12},{9,13},{12,14},{13,15},{14,10},{15,... | collective-permute-start | bytes 393224 | tf_op jit(solution)/shard_map/ppermute | solution.py:39
  18.6 5.7 %collective-permute-start.12 = (bf16[16,4096]{1,0:T(8,128)(2,1)S(1)}, bf16[16,4096]{1,0:T(8,128)(2,1)S(1)}, u32[]{:S(2)}, u32[]{:S(2)}) collective-permute-start(bf16[16,4096]{1,0:T(8,128)(2,1)S(1)} %collective-permute-done.8.refs_9_), channel_id=1, source_target_pairs={{0,2},{1,3},{4,0},{5,1},{8,4},{9,5},{12,8},{13,9},{14,12},{15,13},... | collective-permute-start | bytes 393224 | tf_op jit(solution)/shard_map/ppermute | solution.py:39
  19.8 9.6 %collective-permute-start.13 = (bf16[16,4096]{1,0:T(8,128)(2,1)S(1)}, bf16[16,4096]{1,0:T(8,128)(2,1)S(1)}, u32[]{:S(2)}, u32[]{:S(2)}) collective-permute-start(bf16[16,4096]{1,0:T(8,128)(2,1)S(1)} %collective-permute-done.9.refs_10_), channel_id=1, source_target_pairs={{0,4},{1,5},{4,8},{5,9},{8,12},{9,13},{12,14},{13,15},{14,10},{15,... | collective-permute-start | bytes 393224 | tf_op jit(solution)/shard_map/ppermute | solution.py:39
  21.4 8.0 %collective-permute-start.14 = (bf16[16,4096]{1,0:T(8,128)(2,1)S(1)}, bf16[16,4096]{1,0:T(8,128)(2,1)S(1)}, u32[]{:S(2)}, u32[]{:S(2)}) collective-permute-start(bf16[16,4096]{1,0:T(8,128)(2,1)S(1)} %collective-permute-done.10.refs_11_), channel_id=1, source_target_pairs={{0,2},{1,3},{4,0},{5,1},{8,4},{9,5},{12,8},{13,9},{14,12},{15,13},... | collective-permute-start | bytes 393224 | tf_op jit(solution)/shard_map/ppermute | solution.py:39
  22.7 6.7 %collective-permute-start.15 = (bf16[16,4096]{1,0:T(8,128)(2,1)S(1)}, bf16[16,4096]{1,0:T(8,128)(2,1)S(1)}, u32[]{:S(2)}, u32[]{:S(2)}) collective-permute-start(bf16[16,4096]{1,0:T(8,128)(2,1)S(1)} %collective-permute-done.11.refs_0_), channel_id=1, source_target_pairs={{0,4},{1,5},{4,8},{5,9},{8,12},{9,13},{12,14},{13,15},{14,10},{15,... | collective-permute-start | bytes 393224 | tf_op jit(solution)/shard_map/ppermute | solution.py:39
  24.3 5.1 %collective-permute-start.16 = (bf16[16,4096]{1,0:T(8,128)(2,1)S(1)}, bf16[16,4096]{1,0:T(8,128)(2,1)S(1)}, u32[]{:S(2)}, u32[]{:S(2)}) collective-permute-start(bf16[16,4096]{1,0:T(8,128)(2,1)S(1)} %collective-permute-done.12.refs_1_), channel_id=1, source_target_pairs={{0,2},{1,3},{4,0},{5,1},{8,4},{9,5},{12,8},{13,9},{14,12},{15,13},... | collective-permute-start | bytes 393224 | tf_op jit(solution)/shard_map/ppermute | solution.py:39
  29.4 4.2 %copy-start.1 = (s32[16]{0:T(128)S(1)}, s32[16]{0:T(128)}, u32[]{:S(2)}) copy-start(s32[16]{0:T(128)} %refs_0_) | copy-start | bytes 196
  32.3 1.3 %collective-permute-start.17 = (bf16[128,128]{1,0:T(8,128)(2,1)S(1)}, bf16[128,128]{1,0:T(8,128)(2,1)S(1)}, u32[]{:S(2)}, u32[]{:S(2)}) collective-permute-start(bf16[128,128]{1,0:T(8,128)(2,1)S(1)} %get-tuple-element.142), channel_id=1, source_target_pairs={{0,1},{1,0},{2,3},{3,2},{4,5},{5,4},{6,7},{7,6},{8,9},{9,8},{10,11... | collective-permute-start | bytes 98312 | tf_op jit(solution)/shard_map/ppermute | solution.py:420
  33.6 9.4 %collective-permute-start.1 = (bf16[128,8192]{1,0:T(8,128)(2,1)}, bf16[128,8192]{1,0:T(8,128)(2,1)}, u32[]{:S(2)}, u32[]{:S(2)}) collective-permute-start(bf16[128,8192]{1,0:T(8,128)(2,1)} %get-tuple-element.86.own_ref), channel_id=1, source_target_pairs={{0,1},{1,0},{2,3},{3,2},{4,5},{5,4},{6,7},{7,6},{8,9},{9,8},{10,11... | collective-permute-start | bytes 6291464 | tf_op jit(solution)/shard_map/cond/branch_1_fun/ppermute | solution.py:420
  37.9 40.2 %all-to-all-start.1 = ((bf16[8,96,1024]{2,1,0:T(8,128)(2,1)}), bf16[8,96,1024]{2,1,0:T(8,128)(2,1)S(1)}, u32[]{:S(2)}, u32[]{:S(2)}) async-start(bf16[8,96,1024]{2,1,0:T(8,128)(2,1)} %expand.4), calls=%async_computation.1 | async-start | bytes 3145728 | tf_op jit(solution)/shard_map/cond/branch_1_fun/all_to_all | solution.py:454
where the time goes:
time: 82.1 us; the launch traced here: 80.9 us
  Pallas kernels  34.7 us (42%)
  waiting for transfers between devices  23.5 us (29%)
  starting transfers between devices  21 us (26%)
    pallas_call x1, Pallas kernels, project(): pl.pallas_call(functools.partial(project_kernel, block), grid_spec=pltpu....  20.2 us
    all_to_all x1, waiting for transfers between devices, branch(): lax.all_to_all(products, axis, split_axis=0, concat_axis=0, axis_index_gr...  13.9 us
    ppermute x12, starting transfers between devices, moved(): return lax.ppermute(value, axis, pairs)  13.2 us
    ppermute x12, waiting for transfers between devices, moved(): return lax.ppermute(value, axis, pairs)  9.01 us
    all_to_all x1, starting transfers between devices, branch(): lax.all_to_all(products, axis, split_axis=0, concat_axis=0, axis_index_gr...  5.06 us
    pallas_call x1, Pallas kernels, shrink(): pl.pallas_call(functools.partial(shrink_near_kernel, sizes, [place[1:] fo...  4.63 us
    pallas_call x1, Pallas kernels, expand(): pl.pallas_call(functools.partial(expand_kernel, order, block), grid_spec=...  4.13 us
    pallas_call x1, Pallas kernels, shrink(): pl.pallas_call(functools.partial(shrink_far_kernel, [place[1:] for place...  2.9 us
  transfers between devices with their start and end apart: 18, of which 7 were waited for; matrix products, arithmetic and copies ran while one was open for 1% of the time, Pallas kernels for 39%

commit v1 on v0

--- a/solution.py
+++ b/solution.py
@@ -134,6 +134,7 @@
     chips = tokens_in.shape[0] // rows
     slots = {distance % chips: i for i, distance in enumerate(range(chips // 2 - 1, chips // 2 + 2))}
     copies = down_copies(me[0] % CORES, own_down_ref, other_down_ref, down_vmem, sems)
+    copies.append(pltpu.make_async_copy(shrunk_in, shrunk_ref, sems.at[2]))
     for ref, (column, distance) in zip(piece_refs, places):
         slot = slots[distance % chips]
         copies.append(
@@ -154,7 +155,6 @@
     shrunk = lax.dot_general(
         far_vmem[...], down_vmem[...], (((1,), (1,)), ((), ())), preferred_element_type=jnp.float32
     ).astype(shrunk_ref.dtype)
-    shrunk_ref[...] = shrunk_in[...]
     for i, start in enumerate(starts):
         shrunk_ref[pl.ds(start, rows), :] = shrunk[i * rows : (i + 1) * rows]
     for copy in out_copies:
@@ -204,12 +204,12 @@
         grid_spec=pltpu.PrefetchScalarGridSpec(
             num_scalar_prefetch=1,
             grid=(1,),
-            in_specs=[ANY_SPEC, whole(shrunk_shape.shape)] + [ANY_SPEC] * 8,
+            in_specs=[ANY_SPEC] * 10,
             out_specs=[ANY_SPEC, whole(shrunk_shape.shape)],
             scratch_shapes=[
                 pltpu.VMEM((3 * block, width), jnp.bfloat16),
                 down_vmem,
-                pltpu.SemaphoreType.DMA((11,)),
+                pltpu.SemaphoreType.DMA((12,)),
             ],
         ),
         out_shape=[tokens_shape, shrunk_shape],
@@ -220,7 +220,8 @@
     return tokens, shrunk, held, choice
 
 
-def expand_kernel(order, block, counts, me, held_ref, own_ref, other_ref, keep_ref, got_ref, out_ref, maps_vmem, out_vmem, sems):
+def expand_kernel(order, block, counts, me, held_hbm, own_hbm, other_hbm, keep_ref, got_ref, out_ref, *scratch):
+    held_ref, own_ref, other_ref, maps_vmem, out_vmem, sems = scratch
     chips, slots, units = out_vmem.shape
     most = held_ref.shape[1]
     ranks = keep_ref.shape[0]
@@ -238,8 +239,14 @@
                     sems.at[len(copies)],
                 )
             )
-    for copy in copies:
+    small = [
+        pltpu.make_async_copy(ref, held, sems.at[3 * chips + i])
+        for i, (ref, held) in enumerate(((held_hbm, held_ref), (own_hbm, own_ref), (other_hbm, other_ref)))
+    ]
+    for copy in small + copies:
         copy.start()
+    for copy in small:
+        copy.wait()
 
     wanted = held_ref[pl.ds(chip, 1), :]
     index = lax.broadcasted_iota(jnp.int32, (own_ref.shape[0], most), 0)
@@ -256,14 +263,14 @@
         end = first + counts[chip * adapters + a]
         mine += ((adapter == a) & (slot >= first) & (slot < end)).astype(jnp.int32)
         first = end
-    shrunk = jnp.where(mine > 0, picked, 0.0).astype(jnp.bfloat16)[:slots]
+    shrunk = jnp.where(mine > 0, ADAPTER_SCALE * picked, 0.0).astype(jnp.bfloat16)[:slots]
 
     out_copies = []
     for c in range(chips):
         copies[2 * c].wait()
         copies[2 * c + 1].wait()
         product = jnp.dot(shrunk, maps_vmem[c], preferred_element_type=jnp.float32)
-        out_vmem[c] = (ADAPTER_SCALE * product).astype(out_vmem.dtype)
+        out_vmem[c] = product.astype(out_vmem.dtype)
         out_copies.append(pltpu.make_async_copy(out_vmem.at[c], out_ref.at[c], sems.at[2 * chips + c]))
         out_copies[-1].start()
     for copy in out_copies:
@@ -275,24 +282,20 @@
     chips, most = held.shape
     units = columns // chips // CORES
     rows, ranks_all = own_shrunk.shape
-    shrunk_spec = pl.BlockSpec((rows, ranks_all), lambda i, s, t: (0, 0))
     return pl.pallas_call(
         functools.partial(expand_kernel, order, block),
         grid_spec=pltpu.PrefetchScalarGridSpec(
             num_scalar_prefetch=2,
             grid=(1,),
-            in_specs=[
-                pl.BlockSpec((chips, most), lambda i, s, t: (0, 0)),
-                shrunk_spec,
-                shrunk_spec,
-                ANY_SPEC,
-                ANY_SPEC,
-            ],
+            in_specs=[ANY_SPEC] * 5,
             out_specs=ANY_SPEC,
             scratch_shapes=[
+                pltpu.VMEM((chips, most), jnp.int32),
+                pltpu.VMEM((rows, ranks_all), jnp.bfloat16),
+                pltpu.VMEM((rows, ranks_all), jnp.bfloat16),
                 pltpu.VMEM((chips, ranks_all, units), jnp.bfloat16),
                 pltpu.VMEM((chips, slots, units), jnp.bfloat16),
-                pltpu.SemaphoreType.DMA((3 * chips,)),
+                pltpu.SemaphoreType.DMA((3 * chips + 3,)),
             ],
         ),
         out_shape=pltpu.HBM((chips, slots, units), jnp.bfloat16),

time: 82.1 us -> 75.8 us (0.923)
  waiting for transfers between devices: 23.5 us -> 18.1 us
    all_to_all x1, waiting for transfers between devices: 13.9 us -> 8.51 us  [branch(): lax.all_to_all(products, axis, split_axis=0, concat_axis=0, axis_index_gr...]
  transfers between devices with their start and end apart: 18 -> 18, of which waited for: 7 -> 7; matrix products, arithmetic and copies ran while one was open for 1% -> 1% of each run, Pallas kernels for 39% -> 41%
where the time goes in v1:
time: 75.8 us; the launch traced here: 75.3 us
  Pallas kernels  34 us (45%)
  starting transfers between devices  21 us (28%)
  waiting for transfers between devices  18.1 us (24%)
  other arithmetic  0.97 us (1%)
    pallas_call x1, Pallas kernels, project(): pl.pallas_call(functools.partial(project_kernel, block), grid_spec=pltpu....  20.2 us
    ppermute x12, starting transfers between devices, moved(): return lax.ppermute(value, axis, pairs)  13.2 us
    ppermute x12, waiting for transfers between devices, moved(): return lax.ppermute(value, axis, pairs)  9.01 us
    all_to_all x1, waiting for transfers between devices, branch(): lax.all_to_all(products, axis, split_axis=0, concat_axis=0, axis_index_gr...  8.51 us
    all_to_all x1, starting transfers between devices, branch(): lax.all_to_all(products, axis, split_axis=0, concat_axis=0, axis_index_gr...  5.07 us
    pallas_call x1, Pallas kernels, shrink(): pl.pallas_call(functools.partial(shrink_near_kernel, sizes, [place[1:] fo...  4.63 us
    pallas_call x1, Pallas kernels, expand(): pl.pallas_call(functools.partial(expand_kernel, order, block), grid_spec=...  4.07 us
    pallas_call x1, Pallas kernels, combine(): pl.pallas_call(combine_kernel, grid=(units // tile,), in_specs=[pl.BlockS...  2.78 us
  transfers between devices with their start and end apart: 18, of which 7 were waited for; matrix products, arithmetic and copies ran while one was open for 1% of the time, Pallas kernels for 41%

profile of v1, /device:TPU:0, one launch (start us, length us, event | category | flops | bytes accessed | tf_op | source)
XLA Modules:
  0.0 75.3 jit_solution(15400263490036717915)
XLA Ops:
  0.0 3.0 %collective-permute-start.5 = (bf16[16,8192]{1,0:T(8,128)(2,1)}, bf16[16,8192]{1,0:T(8,128)(2,1)S(1)}, u32[]{:S(2)}, u32[]{:S(2)}) collective-permute-start(bf16[16,8192]{1,0:T(8,128)(2,1)} %refs_5_.1), channel_id=1, source_target_pairs={{0,4},{1,5},{4,8},{5,9},{8,12},{9,13},{12,14},{13,15},{14,10},{15,... | collective-permute-start | bytes 786440 | tf_op jit(solution)/shard_map/ppermute | solution.py:39
  3.0 1.9 %collective-permute-start.4 = (s32[16]{0:T(128)}, s32[16]{0:T(128)S(1)}, u32[]{:S(2)}, u32[]{:S(2)}) collective-permute-start(s32[16]{0:T(128)} %refs_0_), channel_id=1, source_target_pairs={{0,16},{16,0},{1,17},{17,1},{2,18},{18,2},{3,19},{19,3},{4,20},{20... | collective-permute-start | bytes 200 | tf_op jit(solution)/shard_map/ppermute | solution.py:432
  5.0 0.5 collective-permute-start.18
  5.5 4.0 %collective-permute-done.5.refs_6_ = bf16[16,8192]{1,0:T(8,128)(2,1)S(1)} collective-permute-done((bf16[16,8192]{1,0:T(8,128)(2,1)}, bf16[16,8192]{1,0:T(8,128)(2,1)S(1)}, u32[]{:S(2)}, u32[]{:S(2)}) %collective-permute-start.5) | collective-permute-done | bytes 262176 | tf_op jit(solution)/shard_map/ppermute | solution.py:39
  9.5 1.5 %collective-permute-done.6.refs_7_ = bf16[16,8192]{1,0:T(8,128)(2,1)S(1)} collective-permute-done((bf16[16,8192]{1,0:T(8,128)(2,1)}, bf16[16,8192]{1,0:T(8,128)(2,1)S(1)}, u32[]{:S(2)}, u32[]{:S(2)}) %collective-permute-start.6) | collective-permute-done | bytes 262176 | tf_op jit(solution)/shard_map/ppermute | solution.py:39
  11.0 1.6 %collective-permute-start.7 = (bf16[16,4096]{1,0:T(8,128)(2,1)S(1)}, bf16[16,4096]{1,0:T(8,128)(2,1)S(1)}, u32[]{:S(2)}, u32[]{:S(2)}) collective-permute-start(bf16[16,4096]{1,0:T(8,128)(2,1)S(1)} %get-tuple-element.133), channel_id=1, source_target_pairs={{0,4},{1,5},{4,8},{5,9},{8,12},{9,13},{12,14},{13,15},{14,10},{15,... | collective-permute-start | bytes 393224 | tf_op jit(solution)/shard_map/ppermute | solution.py:39
  12.7 0.4 collective-permute-start.8
  13.1 1.6 %collective-permute-start.9 = (bf16[16,4096]{1,0:T(8,128)(2,1)S(1)}, bf16[16,4096]{1,0:T(8,128)(2,1)S(1)}, u32[]{:S(2)}, u32[]{:S(2)}) collective-permute-start(bf16[16,4096]{1,0:T(8,128)(2,1)S(1)} %get-tuple-element.135), channel_id=1, source_target_pairs={{0,4},{1,5},{4,8},{5,9},{8,12},{9,13},{12,14},{13,15},{14,10},{15,... | collective-permute-start | bytes 393224 | tf_op jit(solution)/shard_map/ppermute | solution.py:39
  14.7 0.4 collective-permute-start.10
  15.2 1.9 %collective-permute-done.7.refs_8_ = bf16[16,4096]{1,0:T(8,128)(2,1)S(1)} collective-permute-done((bf16[16,4096]{1,0:T(8,128)(2,1)S(1)}, bf16[16,4096]{1,0:T(8,128)(2,1)S(1)}, u32[]{:S(2)}, u32[]{:S(2)}) %collective-permute-start.7) | collective-permute-done | bytes 131104 | tf_op jit(solution)/shard_map/ppermute | solution.py:39
  17.0 1.6 %collective-permute-start.11 = (bf16[16,4096]{1,0:T(8,128)(2,1)S(1)}, bf16[16,4096]{1,0:T(8,128)(2,1)S(1)}, u32[]{:S(2)}, u32[]{:S(2)}) collective-permute-start(bf16[16,4096]{1,0:T(8,128)(2,1)S(1)} %collective-permute-done.7.refs_8_), channel_id=1, source_target_pairs={{0,4},{1,5},{4,8},{5,9},{8,12},{9,13},{12,14},{13,15},{14,10},{15,... | collective-permute-start | bytes 393224 | tf_op jit(solution)/shard_map/ppermute | solution.py:39
  18.6 0.5 collective-permute-start.12
  19.0 0.8 %collective-permute-done.9.refs_10_ = bf16[16,4096]{1,0:T(8,128)(2,1)S(1)} collective-permute-done((bf16[16,4096]{1,0:T(8,128)(2,1)S(1)}, bf16[16,4096]{1,0:T(8,128)(2,1)S(1)}, u32[]{:S(2)}, u32[]{:S(2)}) %collective-permute-start.9) | collective-permute-done | bytes 131104 | tf_op jit(solution)/shard_map/ppermute | solution.py:39
  19.8 1.6 %collective-permute-start.13 = (bf16[16,4096]{1,0:T(8,128)(2,1)S(1)}, bf16[16,4096]{1,0:T(8,128)(2,1)S(1)}, u32[]{:S(2)}, u32[]{:S(2)}) collective-permute-start(bf16[16,4096]{1,0:T(8,128)(2,1)S(1)} %collective-permute-done.9.refs_10_), channel_id=1, source_target_pairs={{0,4},{1,5},{4,8},{5,9},{8,12},{9,13},{12,14},{13,15},{14,10},{15,... | collective-permute-start | bytes 393224 | tf_op jit(solution)/shard_map/ppermute | solution.py:39
  21.4 0.5 collective-permute-start.14
  21.8 0.9 %collective-permute-done.11.refs_0_ = bf16[16,4096]{1,0:T(8,128)(2,1)S(1)} collective-permute-done((bf16[16,4096]{1,0:T(8,128)(2,1)S(1)}, bf16[16,4096]{1,0:T(8,128)(2,1)S(1)}, u32[]{:S(2)}, u32[]{:S(2)}) %collective-permute-start.11) | collective-permute-done | bytes 131104 | tf_op jit(solution)/shard_map/ppermute | solution.py:39
  22.7 1.6 %collective-permute-start.15 = (bf16[16,4096]{1,0:T(8,128)(2,1)S(1)}, bf16[16,4096]{1,0:T(8,128)(2,1)S(1)}, u32[]{:S(2)}, u32[]{:S(2)}) collective-permute-start(bf16[16,4096]{1,0:T(8,128)(2,1)S(1)} %collective-permute-done.11.refs_0_), channel_id=1, source_target_pairs={{0,4},{1,5},{4,8},{5,9},{8,12},{9,13},{12,14},{13,15},{14,10},{15,... | collective-permute-start | bytes 393224 | tf_op jit(solution)/shard_map/ppermute | solution.py:39
  24.3 0.5 collective-permute-start.16
  24.7 4.6 %shrink_near.1 = (bf16[128,8192]{1,0:T(8,128)(2,1)}, bf16[128,128]{1,0:T(8,128)(2,1)S(1)}, s32[8,128]{1,0:T(8,128)S(1)}, s32[1]{0:T(128)}) custom-call(s32[1]{0:T(128)} %bitcast.4.me, s32[16]{0:T(128)} %refs_0_, s32[16]{0:T(128)S(1)} %collective-permute-done.4.refs_1_, s32[1,256]{1,0:T(1,128)} %bitcast.20, bf16[64,8192]{1,0:T(8,128)(2,1)} %bitcast.17, ...), custom_call_target="tpu_custom_call" | custom-call | tf_op jit(solution)/shard_map/shrink_near/pallas_call | solution.py:180
  29.4 2.3 %shrink_far.1 = (bf16[128,8192]{1,0:T(8,128)(2,1)}, bf16[128,128]{1,0:T(8,128)(2,1)S(1)}) custom-call(s32[1]{0:T(128)} %bitcast.4.me, bf16[128,8192]{1,0:T(8,128)(2,1)} %get-tuple-element.138.tokens_in, bf16[128,128]{1,0:T(8,128)(2,1)S(1)} %get-tuple-element.139.shrunk_in, bf16[64,8192]{1,0:T(8,128)(2,1)} %bitcast.18, ...), custom_call_target="tpu_custom_call", output_to_operand_aliasing={{0}: (1, {})} | custom-call | tf_op jit(solution)/shard_map/shrink_far/pallas_call | solution.py:202
  31.8 0.1 collective-permute-start.17
  32.5 0.5 collective-permute-done.17
  33.0 42.3 %conditional.1 = (bf16[256,1024]{1,0:T(8,128)(2,1)}) conditional(s32[]{:T(128)} %bitcast.7, (bf16[128,8192]{1,0:T(8,128)(2,1)}, s32[8,128]{1,0:T(8,128)S(1)}, s32[1]{0:T(128)}, bf16[8192,1024]{1,0:T(8,128)(2,1)}, bf16[8192,1024]{1,0:T(8,128)(2,1)}, /*index=5*/s32[16]{0:T(128)S(1)}, bf16[128,128]{1,0:T(8,128)(2,1)S(1)}, ...), branch_computations={%region_0.0_spmd, %region_1.0_spmd, %region_2.0_spmd} | conditional | flops 9395765248 | bytes 64833132 | solution.py:469
  33.0 0.2 collective-permute-start
  33.2 4.1 %expand.3 = bf16[8,80,1024]{2,1,0:T(8,128)(2,1)} custom-call(s32[16]{0:T(128)S(1)} %get-tuple-element.80.counts, s32[1]{0:T(128)} %get-tuple-element.74.me, s32[8,128]{1,0:T(8,128)S(1)} %get-tuple-element.71.held_hbm, bf16[128,128]{1,0:T(8,128)(2,1)S(1)} %get-tuple-element.81.own_hbm, bf16[128,128]{1,0:T(8,128)(2,1)S(1)} %get-tuple-element.82.other_hbm, ...), custom_call_target="tpu_custom_call" | custom-call | flops 167772160 | bytes 3407872 | tf_op jit(solution)/shard_map/cond/branch_0_fun/expand/pallas_call | solution.py:285
  37.3 5.1 %all-to-all-start = ((bf16[8,80,1024]{2,1,0:T(8,128)(2,1)}), bf16[8,80,1024]{2,1,0:T(8,128)(2,1)S(1)}, u32[]{:S(2)}, u32[]{:S(2)}) async-start(bf16[8,80,1024]{2,1,0:T(8,128)(2,1)} %expand.3), calls=%async_computation | async-start | bytes 2621440 | tf_op jit(solution)/shard_map/cond/branch_0_fun/all_to_all | solution.py:457
  42.4 0.1 eq.19
  42.5 1.0 %fusion.pick_ref = bf16[256,640]{1,0:T(8,128)(2,1)} fusion(s32[640]{0:T(1024)S(1)} %eq.19), kind=kLoop, calls=%fused_computation.1 | loop fusion | flops 327680 | bytes 330240 | tf_op jit(solution)/shard_map/cond/branch_0_fun/convert_element_type | solution.py:462
  43.5 0.3 copy-done
  43.8 20.2 %project.3 = (f32[256,1024]{1,0:T(8,128)}, f32[256,1024]{1,0:T(8,128)}) custom-call(s32[1]{0:T(128)} %get-tuple-element.74.me, bf16[8192,1024]{1,0:T(8,128)(2,1)} %get-tuple-element.150.gate_weight_ref, bf16[8192,1024]{1,0:T(8,128)(2,1)} %get-tuple-element.153.up_weight_ref, bf16[128,8192]{1,0:T(8,128)(2,1)} %get-tuple-element.70.own_ref, ...), custom_call_target="tpu_custom_call" | custom-call | flops 8589934592 | bytes 37748736 | tf_op jit(solution)/shard_map/cond/branch_0_fun/project/pallas_call | solution.py:349
  64.0 8.5 %all-to-all-done = bf16[8,80,1024]{2,1,0:T(8,128)(2,1)S(1)} async-done(((bf16[8,80,1024]{2,1,0:T(8,128)(2,1)}), bf16[8,80,1024]{2,1,0:T(8,128)(2,1)S(1)}, u32[]{:S(2)}, u32[]{:S(2)}) %all-to-all-start) | async-done | bytes 1310752 | tf_op jit(solution)/shard_map/cond/branch_0_fun/all_to_all | solution.py:457
  72.5 2.8 %combine.3 = bf16[256,1024]{1,0:T(8,128)(2,1)} custom-call(bf16[256,640]{1,0:T(8,128)(2,1)} %fusion.pick_ref, f32[256,1024]{1,0:T(8,128)} %get-tuple-element.78.gate_ref, f32[256,1024]{1,0:T(8,128)} %get-tuple-element.79.up_ref, bf16[640,1024]{1,0:T(8,128)(2,1)S(1)} %bitcast.11), custom_call_target="tpu_custom_call" | custom-call | flops 335544320 | bytes 2621440 | tf_op jit(solution)/shard_map/cond/branch_0_fun/combine/pallas_call | solution.py:382
  (20 shorter events, 0.1 us)
Async XLA Ops:
  0.0 9.5 %collective-permute-start.5 = (bf16[16,8192]{1,0:T(8,128)(2,1)}, bf16[16,8192]{1,0:T(8,128)(2,1)S(1)}, u32[]{:S(2)}, u32[]{:S(2)}) collective-permute-start(bf16[16,8192]{1,0:T(8,128)(2,1)} %refs_5_.1), channel_id=1, source_target_pairs={{0,4},{1,5},{4,8},{5,9},{8,12},{9,13},{12,14},{13,15},{14,10},{15,... | collective-permute-start | bytes 786440 | tf_op jit(solution)/shard_map/ppermute | solution.py:39
  3.0 8.0 %collective-permute-start.6 = (bf16[16,8192]{1,0:T(8,128)(2,1)}, bf16[16,8192]{1,0:T(8,128)(2,1)S(1)}, u32[]{:S(2)}, u32[]{:S(2)}) collective-permute-start(bf16[16,8192]{1,0:T(8,128)(2,1)} %refs_5_.1), channel_id=1, source_target_pairs={{0,2},{1,3},{4,0},{5,1},{8,4},{9,5},{12,8},{13,9},{14,12},{15,13},... | collective-permute-start | bytes 786440 | tf_op jit(solution)/shard_map/ppermute | solution.py:39
  3.0 8.0 %collective-permute-start.4 = (s32[16]{0:T(128)}, s32[16]{0:T(128)S(1)}, u32[]{:S(2)}, u32[]{:S(2)}) collective-permute-start(s32[16]{0:T(128)} %refs_0_), channel_id=1, source_target_pairs={{0,16},{16,0},{1,17},{17,1},{2,18},{18,2},{3,19},{19,3},{4,20},{20... | collective-permute-start | bytes 200 | tf_op jit(solution)/shard_map/ppermute | solution.py:432
  5.0 6.1 %collective-permute-start.3 = (bf16[64,8192]{1,0:T(8,128)(2,1)}, bf16[64,8192]{1,0:T(8,128)(2,1)S(1)}, u32[]{:S(2)}, u32[]{:S(2)}) collective-permute-start(bf16[64,8192]{1,0:T(8,128)(2,1)} %bitcast.16), channel_id=1, source_target_pairs={{0,1},{1,0},{2,3},{3,2},{4,5},{5,4},{6,7},{7,6},{8,9},{9,8},{10,11... | collective-permute-start | bytes 3145736 | tf_op jit(solution)/shard_map/ppermute | solution.py:423
  5.0 28.1 %collective-permute-start.18 = (bf16[64,16384]{1,0:T(8,128)(2,1)}, bf16[64,16384]{1,0:T(8,128)(2,1)}, u32[]{:S(2)}, u32[]{:S(2)}) collective-permute-start(bf16[64,16384]{1,0:T(8,128)(2,1)} %bitcast.12), channel_id=1, source_target_pairs={{0,1},{1,0},{2,3},{3,2},{4,5},{5,4},{6,7},{7,6},{8,9},{9,8},{10,11... | collective-permute-start | bytes 6291464 | tf_op jit(solution)/shard_map/ppermute | solution.py:423
  11.0 6.0 %collective-permute-start.7 = (bf16[16,4096]{1,0:T(8,128)(2,1)S(1)}, bf16[16,4096]{1,0:T(8,128)(2,1)S(1)}, u32[]{:S(2)}, u32[]{:S(2)}) collective-permute-start(bf16[16,4096]{1,0:T(8,128)(2,1)S(1)} %get-tuple-element.133), channel_id=1, source_target_pairs={{0,4},{1,5},{4,8},{5,9},{8,12},{9,13},{12,14},{13,15},{14,10},{15,... | collective-permute-start | bytes 393224 | tf_op jit(solution)/shard_map/ppermute | solution.py:39
  12.7 5.9 %collective-permute-start.8 = (bf16[16,4096]{1,0:T(8,128)(2,1)S(1)}, bf16[16,4096]{1,0:T(8,128)(2,1)S(1)}, u32[]{:S(2)}, u32[]{:S(2)}) collective-permute-start(bf16[16,4096]{1,0:T(8,128)(2,1)S(1)} %get-tuple-element.134), channel_id=1, source_target_pairs={{0,2},{1,3},{4,0},{5,1},{8,4},{9,5},{12,8},{13,9},{14,12},{15,13},... | collective-permute-start | bytes 393224 | tf_op jit(solution)/shard_map/ppermute | solution.py:39
  13.1 6.7 %collective-permute-start.9 = (bf16[16,4096]{1,0:T(8,128)(2,1)S(1)}, bf16[16,4096]{1,0:T(8,128)(2,1)S(1)}, u32[]{:S(2)}, u32[]{:S(2)}) collective-permute-start(bf16[16,4096]{1,0:T(8,128)(2,1)S(1)} %get-tuple-element.135), channel_id=1, source_target_pairs={{0,4},{1,5},{4,8},{5,9},{8,12},{9,13},{12,14},{13,15},{14,10},{15,... | collective-permute-start | bytes 393224 | tf_op jit(solution)/shard_map/ppermute | solution.py:39
  14.7 6.7 %collective-permute-start.10 = (bf16[16,4096]{1,0:T(8,128)(2,1)S(1)}, bf16[16,4096]{1,0:T(8,128)(2,1)S(1)}, u32[]{:S(2)}, u32[]{:S(2)}) collective-permute-start(bf16[16,4096]{1,0:T(8,128)(2,1)S(1)} %get-tuple-element.136), channel_id=1, source_target_pairs={{0,2},{1,3},{4,0},{5,1},{8,4},{9,5},{12,8},{13,9},{14,12},{15,13},... | collective-permute-start | bytes 393224 | tf_op jit(solution)/shard_map/ppermute | solution.py:39
  17.0 5.7 %collective-permute-start.11 = (bf16[16,4096]{1,0:T(8,128)(2,1)S(1)}, bf16[16,4096]{1,0:T(8,128)(2,1)S(1)}, u32[]{:S(2)}, u32[]{:S(2)}) collective-permute-start(bf16[16,4096]{1,0:T(8,128)(2,1)S(1)} %collective-permute-done.7.refs_8_), channel_id=1, source_target_pairs={{0,4},{1,5},{4,8},{5,9},{8,12},{9,13},{12,14},{13,15},{14,10},{15,... | collective-permute-start | bytes 393224 | tf_op jit(solution)/shard_map/ppermute | solution.py:39
  18.6 5.7 %collective-permute-start.12 = (bf16[16,4096]{1,0:T(8,128)(2,1)S(1)}, bf16[16,4096]{1,0:T(8,128)(2,1)S(1)}, u32[]{:S(2)}, u32[]{:S(2)}) collective-permute-start(bf16[16,4096]{1,0:T(8,128)(2,1)S(1)} %collective-permute-done.8.refs_9_), channel_id=1, source_target_pairs={{0,2},{1,3},{4,0},{5,1},{8,4},{9,5},{12,8},{13,9},{14,12},{15,13},... | collective-permute-start | bytes 393224 | tf_op jit(solution)/shard_map/ppermute | solution.py:39
  19.8 9.6 %collective-permute-start.13 = (bf16[16,4096]{1,0:T(8,128)(2,1)S(1)}, bf16[16,4096]{1,0:T(8,128)(2,1)S(1)}, u32[]{:S(2)}, u32[]{:S(2)}) collective-permute-start(bf16[16,4096]{1,0:T(8,128)(2,1)S(1)} %collective-permute-done.9.refs_10_), channel_id=1, source_target_pairs={{0,4},{1,5},{4,8},{5,9},{8,12},{9,13},{12,14},{13,15},{14,10},{15,... | collective-permute-start | bytes 393224 | tf_op jit(solution)/shard_map/ppermute | solution.py:39
  21.4 8.0 %collective-permute-start.14 = (bf16[16,4096]{1,0:T(8,128)(2,1)S(1)}, bf16[16,4096]{1,0:T(8,128)(2,1)S(1)}, u32[]{:S(2)}, u32[]{:S(2)}) collective-permute-start(bf16[16,4096]{1,0:T(8,128)(2,1)S(1)} %collective-permute-done.10.refs_11_), channel_id=1, source_target_pairs={{0,2},{1,3},{4,0},{5,1},{8,4},{9,5},{12,8},{13,9},{14,12},{15,13},... | collective-permute-start | bytes 393224 | tf_op jit(solution)/shard_map/ppermute | solution.py:39
  22.7 6.7 %collective-permute-start.15 = (bf16[16,4096]{1,0:T(8,128)(2,1)S(1)}, bf16[16,4096]{1,0:T(8,128)(2,1)S(1)}, u32[]{:S(2)}, u32[]{:S(2)}) collective-permute-start(bf16[16,4096]{1,0:T(8,128)(2,1)S(1)} %collective-permute-done.11.refs_0_), channel_id=1, source_target_pairs={{0,4},{1,5},{4,8},{5,9},{8,12},{9,13},{12,14},{13,15},{14,10},{15,... | collective-permute-start | bytes 393224 | tf_op jit(solution)/shard_map/ppermute | solution.py:39
  24.3 5.1 %collective-permute-start.16 = (bf16[16,4096]{1,0:T(8,128)(2,1)S(1)}, bf16[16,4096]{1,0:T(8,128)(2,1)S(1)}, u32[]{:S(2)}, u32[]{:S(2)}) collective-permute-start(bf16[16,4096]{1,0:T(8,128)(2,1)S(1)} %collective-permute-done.12.refs_1_), channel_id=1, source_target_pairs={{0,2},{1,3},{4,0},{5,1},{8,4},{9,5},{12,8},{13,9},{14,12},{15,13},... | collective-permute-start | bytes 393224 | tf_op jit(solution)/shard_map/ppermute | solution.py:39
  29.4 3.6 %copy-start.1 = (s32[16]{0:T(128)S(1)}, s32[16]{0:T(128)}, u32[]{:S(2)}) copy-start(s32[16]{0:T(128)} %refs_0_) | copy-start | bytes 196
  31.8 1.3 %collective-permute-start.17 = (bf16[128,128]{1,0:T(8,128)(2,1)S(1)}, bf16[128,128]{1,0:T(8,128)(2,1)S(1)}, u32[]{:S(2)}, u32[]{:S(2)}) collective-permute-start(bf16[128,128]{1,0:T(8,128)(2,1)S(1)} %get-tuple-element.142), channel_id=1, source_target_pairs={{0,1},{1,0},{2,3},{3,2},{4,5},{5,4},{6,7},{7,6},{8,9},{9,8},{10,11... | collective-permute-start | bytes 98312 | tf_op jit(solution)/shard_map/ppermute | solution.py:423
  33.0 9.3 %collective-permute-start = (bf16[128,8192]{1,0:T(8,128)(2,1)}, bf16[128,8192]{1,0:T(8,128)(2,1)S(1)}, u32[]{:S(2)}, u32[]{:S(2)}) collective-permute-start(bf16[128,8192]{1,0:T(8,128)(2,1)} %get-tuple-element.70.own_ref), channel_id=1, source_target_pairs={{0,1},{1,0},{2,3},{3,2},{4,5},{5,4},{6,7},{7,6},{8,9},{9,8},{10,11... | collective-permute-start | bytes 6291464 | tf_op jit(solution)/shard_map/cond/branch_0_fun/ppermute | solution.py:423
  37.3 35.2 %all-to-all-start = ((bf16[8,80,1024]{2,1,0:T(8,128)(2,1)}), bf16[8,80,1024]{2,1,0:T(8,128)(2,1)S(1)}, u32[]{:S(2)}, u32[]{:S(2)}) async-start(bf16[8,80,1024]{2,1,0:T(8,128)(2,1)} %expand.3), calls=%async_computation | async-start | bytes 2621440 | tf_op jit(solution)/shard_map/cond/branch_0_fun/all_to_all | solution.py:457
  42.4 1.4 %copy-start = (bf16[128,8192]{1,0:T(8,128)(2,1)}, bf16[128,8192]{1,0:T(8,128)(2,1)S(1)}, u32[]{:S(2)}) copy-start(bf16[128,8192]{1,0:T(8,128)(2,1)S(1)} %collective-permute-done.other_ref) | copy-start | bytes 6291460 | tf_op jit(solution)/shard_map/cond

commit v2 on v1

--- a/solution.py
+++ b/solution.py
@@ -9,7 +9,7 @@
 
 ADAPTER_SCALE = 0.5
 ROWS_PER_LIMIT = 64
-SLOT_SIZES = (80, 96)
+SLOT_SIZES = (72, 80, 88, 104)
 CORES = 2
 MIB = 1024 * 1024
 
@@ -222,8 +222,9 @@
 
 def expand_kernel(order, block, counts, me, held_hbm, own_hbm, other_hbm, keep_ref, got_ref, out_ref, *scratch):
     held_ref, own_ref, other_ref, maps_vmem, out_vmem, sems = scratch
-    chips, slots, units = out_vmem.shape
-    most = held_ref.shape[1]
+    chips, most = held_ref.shape
+    slots = out_vmem.shape[0] // chips
+    units = out_vmem.shape[1]
     ranks = keep_ref.shape[0]
     adapters = counts.shape[0] // chips
     chip = me[0] // CORES
@@ -263,15 +264,18 @@
         end = first + counts[chip * adapters + a]
         mine += ((adapter == a) & (slot >= first) & (slot < end)).astype(jnp.int32)
         first = end
-    shrunk = jnp.where(mine > 0, ADAPTER_SCALE * picked, 0.0).astype(jnp.bfloat16)[:slots]
+    shrunk = jnp.where(mine > 0, ADAPTER_SCALE * picked, 0.0)[:slots].astype(jnp.bfloat16)
 
     out_copies = []
-    for c in range(chips):
-        copies[2 * c].wait()
-        copies[2 * c + 1].wait()
-        product = jnp.dot(shrunk, maps_vmem[c], preferred_element_type=jnp.float32)
-        out_vmem[c] = product.astype(out_vmem.dtype)
-        out_copies.append(pltpu.make_async_copy(out_vmem.at[c], out_ref.at[c], sems.at[2 * chips + c]))
+    for c in range(0, chips, 2):
+        products = []
+        for i in (c, c + 1):
+            copies[2 * i].wait()
+            copies[2 * i + 1].wait()
+            products.append(jnp.dot(shrunk, maps_vmem[i], preferred_element_type=jnp.float32))
+        part = pl.ds(c * slots, 2 * slots)
+        out_vmem[part, :] = jnp.concatenate(products, axis=0).astype(out_vmem.dtype)
+        out_copies.append(pltpu.make_async_copy(out_vmem.at[part], out_ref.at[part], sems.at[2 * chips + c]))
         out_copies[-1].start()
     for copy in out_copies:
         copy.wait()
@@ -294,11 +298,11 @@
                 pltpu.VMEM((rows, ranks_all), jnp.bfloat16),
                 pltpu.VMEM((rows, ranks_all), jnp.bfloat16),
                 pltpu.VMEM((chips, ranks_all, units), jnp.bfloat16),
-                pltpu.VMEM((chips, slots, units), jnp.bfloat16),
+                pltpu.VMEM((chips * slots, units), jnp.bfloat16),
                 pltpu.SemaphoreType.DMA((3 * chips + 3,)),
             ],
         ),
-        out_shape=pltpu.HBM((chips, slots, units), jnp.bfloat16),
+        out_shape=pltpu.HBM((chips * slots, units), jnp.bfloat16),
         compiler_params=pltpu.CompilerParams(vmem_limit_bytes=16 * MIB),
         cost_estimate=pl.CostEstimate(
             flops=2 * slots * ranks_all * chips * units,
@@ -462,7 +466,7 @@
             pick = (jnp.arange(rows, dtype=jnp.int32)[:, None] == held_rows).astype(jnp.bfloat16)
             pick, other_tokens = lax.optimization_barrier((pick, other_tokens))
             gate, up = project(me_array, own_tokens, other_tokens, gate_weight, up_weight, block)
-            return combine(pick, gate, up, products.reshape(chips * slots, -1))
+            return combine(pick, gate, up, products)
 
         return branch
 

time: 75.8 us -> 80 us (1.055)
  local copies, waits for them, and re-layouts: 0.5 us -> 2.76 us
  waiting for transfers between devices: 18.1 us -> 19.7 us
    all_to_all x1, waiting for transfers between devices: 8.51 us -> 10.1 us  [branch(): lax.all_to_all(products, axis, split_axis=0, concat_axis=0, axis_index_gr...]
    cond x2 -> x6, local copies, waits for them, and re-layouts: 0.35 us -> 1.22 us
  transfers between devices with their start and end apart: 18 -> 18, of which waited for: 7 -> 7; matrix products, arithmetic and copies ran while one was open for 1% -> 3% of each run, Pallas kernels for 41% -> 39%
where the time goes in v2:
time: 80 us; the launch traced here: 79.1 us
  Pallas kernels  34 us (42%)
  starting transfers between devices  21 us (26%)
  waiting for transfers between devices  19.7 us (25%)
  local copies, waits for them, and re-layouts  2.76 us (3%)
  other arithmetic  0.84 us (1%)
    pallas_call x1, Pallas kernels, project(): pl.pallas_call(functools.partial(project_kernel, block), grid_spec=pltpu....  20.1 us
    ppermute x12, starting transfers between devices, moved(): return lax.ppermute(value, axis, pairs)  13.2 us
    all_to_all x1, waiting for transfers between devices, branch(): lax.all_to_all(products, axis, split_axis=0, concat_axis=0, axis_index_gr...  10.1 us
    ppermute x12, waiting for transfers between devices, moved(): return lax.ppermute(value, axis, pairs)  9.01 us
    all_to_all x1, starting transfers between devices, branch(): lax.all_to_all(products, axis, split_axis=0, concat_axis=0, axis_index_gr...  5.12 us
    pallas_call x1, Pallas kernels, shrink(): pl.pallas_call(functools.partial(shrink_near_kernel, sizes, [place[1:] fo...  4.61 us
    pallas_call x1, Pallas kernels, expand(): pl.pallas_call(functools.partial(expand_kernel, order, block), grid_spec=...  4.18 us
    pallas_call x1, Pallas kernels, combine(): pl.pallas_call(combine_kernel, grid=(units // tile,), in_specs=[pl.BlockS...  2.81 us
  transfers between devices with their start and end apart: 18, of which 7 were waited for; matrix products, arithmetic and copies ran while one was open for 3% of the time, Pallas kernels for 39%

profile of v2, /device:TPU:0, one launch (start us, length us, event | category | flops | bytes accessed | tf_op | source)
XLA Modules:
  0.0 79.1 jit_solution(4415736150485241506)
XLA Ops:
  0.0 3.0 %collective-permute-start.7 = (bf16[16,8192]{1,0:T(8,128)(2,1)}, bf16[16,8192]{1,0:T(8,128)(2,1)S(1)}, u32[]{:S(2)}, u32[]{:S(2)}) collective-permute-start(bf16[16,8192]{1,0:T(8,128)(2,1)} %refs_5_.1), channel_id=1, source_target_pairs={{0,4},{1,5},{4,8},{5,9},{8,12},{9,13},{12,14},{13,15},{14,10},{15,... | collective-permute-start | bytes 786440 | tf_op jit(solution)/shard_map/ppermute | solution.py:39
  3.0 1.9 %collective-permute-start.6 = (s32[16]{0:T(128)}, s32[16]{0:T(128)S(1)}, u32[]{:S(2)}, u32[]{:S(2)}) collective-permute-start(s32[16]{0:T(128)} %refs_0_), channel_id=1, source_target_pairs={{0,16},{16,0},{1,17},{17,1},{2,18},{18,2},{3,19},{19,3},{4,20},{20... | collective-permute-start | bytes 200 | tf_op jit(solution)/shard_map/ppermute | solution.py:436
  5.0 0.5 collective-permute-start.20
  5.5 4.0 %collective-permute-done.7.refs_6_ = bf16[16,8192]{1,0:T(8,128)(2,1)S(1)} collective-permute-done((bf16[16,8192]{1,0:T(8,128)(2,1)}, bf16[16,8192]{1,0:T(8,128)(2,1)S(1)}, u32[]{:S(2)}, u32[]{:S(2)}) %collective-permute-start.7) | collective-permute-done | bytes 262176 | tf_op jit(solution)/shard_map/ppermute | solution.py:39
  9.5 1.5 %collective-permute-done.8.refs_7_ = bf16[16,8192]{1,0:T(8,128)(2,1)S(1)} collective-permute-done((bf16[16,8192]{1,0:T(8,128)(2,1)}, bf16[16,8192]{1,0:T(8,128)(2,1)S(1)}, u32[]{:S(2)}, u32[]{:S(2)}) %collective-permute-start.8) | collective-permute-done | bytes 262176 | tf_op jit(solution)/shard_map/ppermute | solution.py:39
  11.0 1.6 %collective-permute-start.9 = (bf16[16,4096]{1,0:T(8,128)(2,1)S(1)}, bf16[16,4096]{1,0:T(8,128)(2,1)S(1)}, u32[]{:S(2)}, u32[]{:S(2)}) collective-permute-start(bf16[16,4096]{1,0:T(8,128)(2,1)S(1)} %get-tuple-element.207), channel_id=1, source_target_pairs={{0,4},{1,5},{4,8},{5,9},{8,12},{9,13},{12,14},{13,15},{14,10},{15,... | collective-permute-start | bytes 393224 | tf_op jit(solution)/shard_map/ppermute | solution.py:39
  12.7 0.4 collective-permute-start.10
  13.1 1.6 %collective-permute-start.11 = (bf16[16,4096]{1,0:T(8,128)(2,1)S(1)}, bf16[16,4096]{1,0:T(8,128)(2,1)S(1)}, u32[]{:S(2)}, u32[]{:S(2)}) collective-permute-start(bf16[16,4096]{1,0:T(8,128)(2,1)S(1)} %get-tuple-element.209), channel_id=1, source_target_pairs={{0,4},{1,5},{4,8},{5,9},{8,12},{9,13},{12,14},{13,15},{14,10},{15,... | collective-permute-start | bytes 393224 | tf_op jit(solution)/shard_map/ppermute | solution.py:39
  14.7 0.4 collective-permute-start.12
  15.2 1.9 %collective-permute-done.9.refs_8_ = bf16[16,4096]{1,0:T(8,128)(2,1)S(1)} collective-permute-done((bf16[16,4096]{1,0:T(8,128)(2,1)S(1)}, bf16[16,4096]{1,0:T(8,128)(2,1)S(1)}, u32[]{:S(2)}, u32[]{:S(2)}) %collective-permute-start.9) | collective-permute-done | bytes 131104 | tf_op jit(solution)/shard_map/ppermute | solution.py:39
  17.0 1.6 %collective-permute-start.13 = (bf16[16,4096]{1,0:T(8,128)(2,1)S(1)}, bf16[16,4096]{1,0:T(8,128)(2,1)S(1)}, u32[]{:S(2)}, u32[]{:S(2)}) collective-permute-start(bf16[16,4096]{1,0:T(8,128)(2,1)S(1)} %collective-permute-done.9.refs_8_), channel_id=1, source_target_pairs={{0,4},{1,5},{4,8},{5,9},{8,12},{9,13},{12,14},{13,15},{14,10},{15,... | collective-permute-start | bytes 393224 | tf_op jit(solution)/shard_map/ppermute | solution.py:39
  18.6 0.5 collective-permute-start.14
  19.0 0.8 collective-permute-done.11.refs_10_
  19.8 1.6 %collective-permute-start.15 = (bf16[16,4096]{1,0:T(8,128)(2,1)S(1)}, bf16[16,4096]{1,0:T(8,128)(2,1)S(1)}, u32[]{:S(2)}, u32[]{:S(2)}) collective-permute-start(bf16[16,4096]{1,0:T(8,128)(2,1)S(1)} %collective-permute-done.11.refs_10_), channel_id=1, source_target_pairs={{0,4},{1,5},{4,8},{5,9},{8,12},{9,13},{12,14},{13,15},{14,10},{15,... | collective-permute-start | bytes 393224 | tf_op jit(solution)/shard_map/ppermute | solution.py:39
  21.4 0.5 collective-permute-start.16
  21.8 0.9 %collective-permute-done.13.refs_0_ = bf16[16,4096]{1,0:T(8,128)(2,1)S(1)} collective-permute-done((bf16[16,4096]{1,0:T(8,128)(2,1)S(1)}, bf16[16,4096]{1,0:T(8,128)(2,1)S(1)}, u32[]{:S(2)}, u32[]{:S(2)}) %collective-permute-start.13) | collective-permute-done | bytes 131104 | tf_op jit(solution)/shard_map/ppermute | solution.py:39
  22.7 1.6 %collective-permute-start.17 = (bf16[16,4096]{1,0:T(8,128)(2,1)S(1)}, bf16[16,4096]{1,0:T(8,128)(2,1)S(1)}, u32[]{:S(2)}, u32[]{:S(2)}) collective-permute-start(bf16[16,4096]{1,0:T(8,128)(2,1)S(1)} %collective-permute-done.13.refs_0_), channel_id=1, source_target_pairs={{0,4},{1,5},{4,8},{5,9},{8,12},{9,13},{12,14},{13,15},{14,10},{15,... | collective-permute-start | bytes 393224 | tf_op jit(solution)/shard_map/ppermute | solution.py:39
  24.3 0.5 collective-permute-start.18
  24.7 4.6 %shrink_near.1 = (bf16[128,8192]{1,0:T(8,128)(2,1)}, bf16[128,128]{1,0:T(8,128)(2,1)S(1)}, s32[8,128]{1,0:T(8,128)S(1)}, s32[1]{0:T(128)}) custom-call(s32[1]{0:T(128)} %bitcast.11.me, s32[16]{0:T(128)} %refs_0_, s32[16]{0:T(128)S(1)} %collective-permute-done.6.refs_1_, s32[1,256]{1,0:T(1,128)} %bitcast.36, bf16[64,8192]{1,0:T(8,128)(2,1)} %bitcast.33, ...), custom_call_target="tpu_custom_call" | custom-call | tf_op jit(solution)/shard_map/shrink_near/pallas_call | solution.py:180
  29.4 2.3 %shrink_far.1 = (bf16[128,8192]{1,0:T(8,128)(2,1)}, bf16[128,128]{1,0:T(8,128)(2,1)S(1)}) custom-call(s32[1]{0:T(128)} %bitcast.11.me, bf16[128,8192]{1,0:T(8,128)(2,1)} %get-tuple-element.212.tokens_in, bf16[128,128]{1,0:T(8,128)(2,1)S(1)} %get-tuple-element.213.shrunk_in, bf16[64,8192]{1,0:T(8,128)(2,1)} %bitcast.34, ...), custom_call_target="tpu_custom_call", output_to_operand_aliasing={{0}: (1, {})} | custom-call | tf_op jit(solution)/shard_map/shrink_far/pallas_call | solution.py:202
  32.4 0.5 collective-permute-done.19
  33.0 46.1 %conditional.1 = (bf16[256,1024]{1,0:T(8,128)(2,1)}) conditional(s32[]{:T(128)} %bitcast.14, (bf16[128,8192]{1,0:T(8,128)(2,1)}, s32[8,128]{1,0:T(8,128)S(1)}, s32[1]{0:T(128)}, bf16[8192,1024]{1,0:T(8,128)(2,1)}, bf16[8192,1024]{1,0:T(8,128)(2,1)}, /*index=5*/s32[16]{0:T(128)S(1)}, bf16[128,128]{1,0:T(8,128)(2,1)S(1)}, ...), branch_computations={%region_0.0_spmd, %region_1.0_spmd, %region_2.0_spmd, %region_3.0_... | conditional | flops 9395765248 | bytes 65654180 | solution.py:473
  33.0 0.6 copy-done.3
  33.6 0.6 copy-done.4
  34.4 4.2 %expand.7 = bf16[704,1024]{1,0:T(8,128)(2,1)} custom-call(s32[16]{0:T(128)S(1)} %get-tuple-element.154.counts, s32[1]{0:T(128)} %get-tuple-element.148.me, s32[8,128]{1,0:T(8,128)S(1)} %get-tuple-element.145.held_hbm, bf16[128,128]{1,0:T(8,128)(2,1)} %copy-done.3, bf16[128,128]{1,0:T(8,128)(2,1)} %copy-done.4, ...), custom_call_target="tpu_custom_call" | custom-call | flops 184549376 | bytes 3538944 | tf_op jit(solution)/shard_map/cond/branch_2_fun/expand/pallas_call | solution.py:289
  38.6 5.1 %all-to-all-start.2 = ((bf16[8,88,1024]{2,1,0:T(8,128)(2,1)}), bf16[8,88,1024]{2,1,0:T(8,128)(2,1)S(1)}, u32[]{:S(2)}, u32[]{:S(2)}) async-start(bf16[8,88,1024]{2,1,0:T(8,128)(2,1)} %bitcast.29), calls=%async_computation.2 | async-start | bytes 2883584 | tf_op jit(solution)/shard_map/cond/branch_2_fun/all_to_all | solution.py:461
  43.7 0.6 fusion.7
  44.3 0.8 stack.12
  45.2 0.8 %fusion.2.pick_ref = bf16[256,704]{1,0:T(8,128)(2,1)} fusion(s32[704]{0:T(1024)S(1)} %eq.57), kind=kLoop, calls=%fused_computation.5 | loop fusion | flops 360448 | bytes 363264 | tf_op jit(solution)/shard_map/cond/branch_2_fun/convert_element_type | solution.py:466
  46.0 20.1 %project.7 = (f32[256,1024]{1,0:T(8,128)}, f32[256,1024]{1,0:T(8,128)}) custom-call(s32[1]{0:T(128)} %get-tuple-element.148.me, bf16[8192,1024]{1,0:T(8,128)(2,1)} %get-tuple-element.230.gate_weight_ref, bf16[8192,1024]{1,0:T(8,128)(2,1)} %get-tuple-element.235.up_weight_ref, bf16[128,8192]{1,0:T(8,128)(2,1)} %get-tuple-element.144.own_ref, ...), custom_call_target="tpu_custom_call" | custom-call | flops 8589934592 | bytes 37748736 | tf_op jit(solution)/shard_map/cond/branch_2_fun/project/pallas_call | solution.py:353
  66.2 10.1 %all-to-all-done.2 = bf16[8,88,1024]{2,1,0:T(8,128)(2,1)S(1)} async-done(((bf16[8,88,1024]{2,1,0:T(8,128)(2,1)}), bf16[8,88,1024]{2,1,0:T(8,128)(2,1)S(1)}, u32[]{:S(2)}, u32[]{:S(2)}) %all-to-all-start.2) | async-done | bytes 1441824 | tf_op jit(solution)/shard_map/cond/branch_2_fun/all_to_all | solution.py:461
  76.3 2.8 %combine.7 = bf16[256,1024]{1,0:T(8,128)(2,1)} custom-call(bf16[256,704]{1,0:T(8,128)(2,1)} %fusion.2.pick_ref, f32[256,1024]{1,0:T(8,128)} %get-tuple-element.152.gate_ref, f32[256,1024]{1,0:T(8,128)} %get-tuple-element.153.up_ref, bf16[704,1024]{1,0:T(8,128)(2,1)S(1)} %bitcast.18), custom_call_target="tpu_custom_call" | custom-call | flops 369098752 | bytes 2621440 | tf_op jit(solution)/shard_map/cond/branch_2_fun/combine/pallas_call | solution.py:386
  (24 shorter events, 0.4 us)
Async XLA Ops:
  0.0 9.5 %collective-permute-start.7 = (bf16[16,8192]{1,0:T(8,128)(2,1)}, bf16[16,8192]{1,0:T(8,128)(2,1)S(1)}, u32[]{:S(2)}, u32[]{:S(2)}) collective-permute-start(bf16[16,8192]{1,0:T(8,128)(2,1)} %refs_5_.1), channel_id=1, source_target_pairs={{0,4},{1,5},{4,8},{5,9},{8,12},{9,13},{12,14},{13,15},{14,10},{15,... | collective-permute-start | bytes 786440 | tf_op jit(solution)/shard_map/ppermute | solution.py:39
  3.0 8.0 %collective-permute-start.8 = (bf16[16,8192]{1,0:T(8,128)(2,1)}, bf16[16,8192]{1,0:T(8,128)(2,1)S(1)}, u32[]{:S(2)}, u32[]{:S(2)}) collective-permute-start(bf16[16,8192]{1,0:T(8,128)(2,1)} %refs_5_.1), channel_id=1, source_target_pairs={{0,2},{1,3},{4,0},{5,1},{8,4},{9,5},{12,8},{13,9},{14,12},{15,13},... | collective-permute-start | bytes 786440 | tf_op jit(solution)/shard_map/ppermute | solution.py:39
  3.0 8.0 %collective-permute-start.6 = (s32[16]{0:T(128)}, s32[16]{0:T(128)S(1)}, u32[]{:S(2)}, u32[]{:S(2)}) collective-permute-start(s32[16]{0:T(128)} %refs_0_), channel_id=1, source_target_pairs={{0,16},{16,0},{1,17},{17,1},{2,18},{18,2},{3,19},{19,3},{4,20},{20... | collective-permute-start | bytes 200 | tf_op jit(solution)/shard_map/ppermute | solution.py:436
  5.0 6.1 %collective-permute-start.5 = (bf16[64,8192]{1,0:T(8,128)(2,1)}, bf16[64,8192]{1,0:T(8,128)(2,1)S(1)}, u32[]{:S(2)}, u32[]{:S(2)}) collective-permute-start(bf16[64,8192]{1,0:T(8,128)(2,1)} %bitcast.32), channel_id=1, source_target_pairs={{0,1},{1,0},{2,3},{3,2},{4,5},{5,4},{6,7},{7,6},{8,9},{9,8},{10,11... | collective-permute-start | bytes 3145736 | tf_op jit(solution)/shard_map/ppermute | solution.py:427
  5.0 28.0 %collective-permute-start.20 = (bf16[64,16384]{1,0:T(8,128)(2,1)}, bf16[64,16384]{1,0:T(8,128)(2,1)}, u32[]{:S(2)}, u32[]{:S(2)}) collective-permute-start(bf16[64,16384]{1,0:T(8,128)(2,1)} %bitcast.21), channel_id=1, source_target_pairs={{0,1},{1,0},{2,3},{3,2},{4,5},{5,4},{6,7},{7,6},{8,9},{9,8},{10,11... | collective-permute-start | bytes 6291464 | tf_op jit(solution)/shard_map/ppermute | solution.py:427
  11.0 6.0 %collective-permute-start.9 = (bf16[16,4096]{1,0:T(8,128)(2,1)S(1)}, bf16[16,4096]{1,0:T(8,128)(2,1)S(1)}, u32[]{:S(2)}, u32[]{:S(2)}) collective-permute-start(bf16[16,4096]{1,0:T(8,128)(2,1)S(1)} %get-tuple-element.207), channel_id=1, source_target_pairs={{0,4},{1,5},{4,8},{5,9},{8,12},{9,13},{12,14},{13,15},{14,10},{15,... | collective-permute-start | bytes 393224 | tf_op jit(solution)/shard_map/ppermute | solution.py:39
  12.7 5.9 %collective-permute-start.10 = (bf16[16,4096]{1,0:T(8,128)(2,1)S(1)}, bf16[16,4096]{1,0:T(8,128)(2,1)S(1)}, u32[]{:S(2)}, u32[]{:S(2)}) collective-permute-start(bf16[16,4096]{1,0:T(8,128)(2,1)S(1)} %get-tuple-element.208), channel_id=1, source_target_pairs={{0,2},{1,3},{4,0},{5,1},{8,4},{9,5},{12,8},{13,9},{14,12},{15,13},... | collective-permute-start | bytes 393224 | tf_op jit(solution)/shard_map/ppermute | solution.py:39
  13.1 6.7 %collective-permute-start.11 = (bf16[16,4096]{1,0:T(8,128)(2,1)S(1)}, bf16[16,4096]{1,0:T(8,128)(2,1)S(1)}, u32[]{:S(2)}, u32[]{:S(2)}) collective-permute-start(bf16[16,4096]{1,0:T(8,128)(2,1)S(1)} %get-tuple-element.209), channel_id=1, source_target_pairs={{0,4},{1,5},{4,8},{5,9},{8,12},{9,13},{12,14},{13,15},{14,10},{15,... | collective-permute-start | bytes 393224 | tf_op jit(solution)/shard_map/ppermute | solution.py:39
  14.7 6.7 %collective-permute-start.12 = (bf16[16,4096]{1,0:T(8,128)(2,1)S(1)}, bf16[16,4096]{1,0:T(8,128)(2,1)S(1)}, u32[]{:S(2)}, u32[]{:S(2)}) collective-permute-start(bf16[16,4096]{1,0:T(8,128)(2,1)S(1)} %get-tuple-element.210), channel_id=1, source_target_pairs={{0,2},{1,3},{4,0},{5,1},{8,4},{9,5},{12,8},{13,9},{14,12},{15,13},... | collective-permute-start | bytes 393224 | tf_op jit(solution)/shard_map/ppermute | solution.py:39
  17.0 5.7 %collective-permute-start.13 = (bf16[16,4096]{1,0:T(8,128)(2,1)S(1)}, bf16[16,4096]{1,0:T(8,128)(2,1)S(1)}, u32[]{:S(2)}, u32[]{:S(2)}) collective-permute-start(bf16[16,4096]{1,0:T(8,128)(2,1)S(1)} %collective-permute-done.9.refs_8_), channel_id=1, source_target_pairs={{0,4},{1,5},{4,8},{5,9},{8,12},{9,13},{12,14},{13,15},{14,10},{15,... | collective-permute-start | bytes 393224 | tf_op jit(solution)/shard_map/ppermute | solution.py:39
  18.6 5.7 %collective-permute-start.14 = (bf16[16,4096]{1,0:T(8,128)(2,1)S(1)}, bf16[16,4096]{1,0:T(8,128)(2,1)S(1)}, u32[]{:S(2)}, u32[]{:S(2)}) collective-permute-start(bf16[16,4096]{1,0:T(8,128)(2,1)S(1)} %collective-permute-done.10.refs_9_), channel_id=1, source_target_pairs={{0,2},{1,3},{4,0},{5,1},{8,4},{9,5},{12,8},{13,9},{14,12},{15,13},... | collective-permute-start | bytes 393224 | tf_op jit(solution)/shard_map/ppermute | solution.py:39
  19.8 9.5 %collective-permute-start.15 = (bf16[16,4096]{1,0:T(8,128)(2,1)S(1)}, bf16[16,4096]{1,0:T(8,128)(2,1)S(1)}, u32[]{:S(2)}, u32[]{:S(2)}) collective-permute-start(bf16[16,4096]{1,0:T(8,128)(2,1)S(1)} %collective-permute-done.11.refs_10_), channel_id=1, source_target_pairs={{0,4},{1,5},{4,8},{5,9},{8,12},{9,13},{12,14},{13,15},{14,10},{15,... | collective-permute-start | bytes 393224 | tf_op jit(solution)/shard_map/ppermute | solution.py:39
  21.4 8.0 %collective-permute-start.16 = (bf16[16,4096]{1,0:T(8,128)(2,1)S(1)}, bf16[16,4096]{1,0:T(8,128)(2,1)S(1)}, u32[]{:S(2)}, u32[]{:S(2)}) collective-permute-start(bf16[16,4096]{1,0:T(8,128)(2,1)S(1)} %collective-permute-done.12.refs_11_), channel_id=1, source_target_pairs={{0,2},{1,3},{4,0},{5,1},{8,4},{9,5},{12,8},{13,9},{14,12},{15,13},... | collective-permute-start | bytes 393224 | tf_op jit(solution)/shard_map/ppermute | solution.py:39
  22.7 6.7 %collective-permute-start.17 = (bf16[16,4096]{1,0:T(8,128)(2,1)S(1)}, bf16[16,4096]{1,0:T(8,128)(2,1)S(1)}, u32[]{:S(2)}, u32[]{:S(2)}) collective-permute-start(bf16[16,4096]{1,0:T(8,128)(2,1)S(1)} %collective-permute-done.13.refs_0_), channel_id=1, source_target_pairs={{0,4},{1,5},{4,8},{5,9},{8,12},{9,13},{12,14},{13,15},{14,10},{15,... | collective-permute-start | bytes 393224 | tf_op jit(solution)/shard_map/ppermute | solution.py:39
  24.3 5.1 %collective-permute-start.18 = (bf16[16,4096]{1,0:T(8,128)(2,1)S(1)}, bf16[16,4096]{1,0:T(8,128)(2,1)S(1)}, u32[]{:S(2)}, u32[]{:S(2)}) collective-permute-start(bf16[16,4096]{1,0:T(8,128)(2,1)S(1)} %collective-permute-done.14.refs_1_), channel_id=1, source_target_pairs={{0,2},{1,3},{4,0},{5,1},{8,4},{9,5},{12,8},{13,9},{14,12},{15,13},... | collective-permute-start | bytes 393224 | tf_op jit(solution)/shard_map/ppermute | solution.py:39
  29.4 3.6 %copy-start.5 = (s32[16]{0:T(128)S(1)}, s32[16]{0:T(128)}, u32[]{:S(2)}) copy-start(s32[16]{0:T(128)} %refs_0_) | copy-start | bytes 196
  31.7 1.3 %collective-permute-start.19 = (bf16[128,128]{1,0:T(8,128)(2,1)S(1)}, bf16[128,128]{1,0:T(8,128)(2,1)S(1)}, u32[]{:S(2)}, u32[]{:S(2)}) collective-permute-start(bf16[128,128]{1,0:T(8,128)(2,1)S(1)} %get-tuple-element.216), channel_id=1, source_target_pairs={{0,1},{1,0},{2,3},{3,2},{4,5},{5,4},{6,7},{7,6},{8,9},{9,8},{10,11... | collective-permute-start | bytes 98312 | tf_op jit(solution)/shard_map/ppermute | solution.py:427
  33.0 0.6 copy-start.3
  33.6 0.6 copy-start.4
  34.2 9.5 %collective-permute-start.2 = (bf16[128,8192]{1,0:T(8,128)(2,1)}, bf16[128,8192]{1,0:T(8,128)(2,1)S(1)}, u32[]{:S(2)}, u32[]{:S(2)}) collective-permute-start(bf16[128,8192]{1,0:T(8,128)(2,1)} %get-tuple-element.144.own_ref), channel_id=1, source_target_pairs={{0,1},{1,0},{2,3},{3,2},{4,5},{5,4},{6,7},{7,6},{8,9},{9,8},{10,11... | collective-permute-start | bytes 6291464 | tf_op jit(solution)/shard_map/cond/branch_2_fun/ppermute | solution.py:427
  38.6 37.7 %all-to-all-start.2 = ((bf16[8,88,1024]{2,1,0:T(8,128)(2,1)}), bf16[8,88,1024]{2,1,0:T(8,128)(2,1)S(1)}, u32[]{:S(2)}, u32[]{:S(2)}) async-start(bf16[8,88,1024]{2,1,0:T(8,128)(2,1)} %bitcast.29), calls=%async_computation.2 | async-start | bytes 2883584 | tf_op jit(solution)/shard_map/cond/branch_2_fun/all_to_all | solution.py:461
  43.7 2.4 %copy-start.2 = (bf16[128,8192]{1,0:T(8,128)(2,1)}, bf16[128,8192]{1,0:T(8,128)(2,1)S(1)}, u32[]{:S(2)}) copy-start(bf16[128,8192]{1,0:T(8,128)(2,1)S(1)} %collective-permute-done.2.other_ref) | copy-start | bytes 6291460 | tf_op jit(solution)/shard_map/cond
